TPU v7x, 256 devices: a whole 4x4x8 slice. The times are simulated.
256 devices in a mesh: lon: 32 (over z, x), lat: 8 (over y, core).
Axes of the slice: x: 4, y: 4, z: 8, core: 2. Of those that a mesh axis runs over, the one named last changes fastest.
Arguments:
- warmth_deviation: float32 [10, 512, 4096], P(None, 'lat', 'lon'), may hold values from -6 to 6
- saltiness_deviation: float32 [10, 512, 4096], P(None, 'lat', 'lon'), may hold values from -6 to 6
- easterly_speed: float32 [10, 512, 4096], P(None, 'lat', 'lon'), may hold values from -6 to 6
- poleward_speed: float32 [10, 512, 4096], P(None, 'lat', 'lon'), may hold values from -6 to 6
- stratum_spans: float32 [10], replicated, may hold values from 0.5 to 2
- water_indicator: int32 [512, 4096], P('lat', 'lon'), may hold values 0 or 1
- opposite_counterpart: int32 [4096], P('lon'), may hold values from 0 to 4095, as said below
- elevation_weights: float32 [512, 4096], P('lat', 'lon'), may hold values from 0.2 to 2
- elevation_anomaly: float32 [512, 4096], P('lat', 'lon'), may hold values from -3 to 17
Outputs:
- new_temperature: float32 [10, 512, 4096], P(None, 'lat', 'lon')
- new_salinity: float32 [10, 512, 4096], P(None, 'lat', 'lon')
- new_zonal: float32 [10, 512, 4096], P(None, 'lat', 'lon')
- new_meridional: float32 [10, 512, 4096], P(None, 'lat', 'lon')
- new_surface: float32 [512, 4096], P('lat', 'lon')
Inputs may be any that keep to these rules, and one draw needn't show every extreme that they name: opposite_counterpart[x] = (h - 1 - x) mod 4096 for a hinge column h chosen by the draw, so opposite_counterpart[opposite_counterpart[x]] = x.
All inputs are finite; a program needn't handle non-finite values. No bound on the sum of `water_indicator` on one device may be relied on, other than what follows from the above.
Results may differ from a plain program's by a relative error of at most 0.0001.
Values sent between devices are 32-bit elements; how exact they have to be, the bound alone decides.
A program may use at most 64 MiB of HBM per device.

v0:
```python
import jax
import jax.numpy as jnp
from jax import lax
from jax.sharding import PartitionSpec as P

ITERS = 3


LINEAR_HEAT = 1.0
SQUARE_HEAT = 0.3
SALT_COEF = 0.8
CROSS_COEF = 0.2
TIME_STEP = 0.1
MIXING = 0.1


def extended_2(cells, sides, width, closed):
    for axis, dim in sides:
        count = lax.axis_size(axis)
        ends = count if closed else count - 1
        head = lax.slice_in_dim(cells, 0, width, axis=dim)
        tail = lax.slice_in_dim(cells, cells.shape[dim] - width, cells.shape[dim], axis=dim)
        cells = jnp.concatenate(
            [
                lax.ppermute(tail, axis, [(i, (i + 1) % count) for i in range(ends)]),
                cells,
                lax.ppermute(head, axis, [((i + 1) % count, i) for i in range(ends)]),
            ],
            axis=dim,
        )
    return cells


def density(heat_part, salt_part):
    return (
        -LINEAR_HEAT * heat_part
        - 0.5 * SQUARE_HEAT * heat_part * heat_part
        + SALT_COEF * salt_part
        - CROSS_COEF * heat_part * salt_part
    )


def pressure(heat_part, salt_part, stratum_spans):
    layers = density(heat_part, salt_part) * stratum_spans[:, None, None]
    return jnp.cumsum(layers, axis=0) - 0.5 * layers


def attach(extended, north, is_top, width):
    keep = extended[..., :-width, :]
    rim = jnp.where(is_top, north, extended[..., -width:, :])
    return jnp.concatenate([keep, rim], axis=-2)


def operate(field, diagonal, wetness, opposite_counterpart, is_top):
    height = field.shape[0]
    cycle_ext = extended_2(field, (("lon", 1),), 1, True)
    row_ext = extended_2(field, (("lat", 0),), 1, False)
    gathered = lax.all_gather(field[height - 1 :, :], "lon", axis=1, tiled=True)
    north_row = jnp.take(gathered, opposite_counterpart, axis=1)
    row_ext = attach(row_ext, north_row, is_top, 1)
    neighbours = cycle_ext[:, 2:] + cycle_ext[:, :-2] + row_ext[2:, :] + row_ext[:-2, :]
    return diagonal * field - wetness * neighbours


def norm_sum(residual, precond):
    return lax.psum(jnp.sum(residual * precond), ("lon", "lat"))


def body(
    warmth_deviation,
    saltiness_deviation,
    easterly_speed,
    poleward_speed,
    stratum_spans,
    water_indicator,
    opposite_counterpart,
    elevation_weights,
    elevation_anomaly,
):
    wetness = water_indicator.astype(jnp.float32)
    is_top = lax.axis_index("lat") == lax.axis_size("lat") - 1
    advected_quantities = jnp.stack([warmth_deviation, saltiness_deviation])
    height = advected_quantities.shape[2]
    along = extended_2(advected_quantities, (("lon", 3),), 2, True)
    across = extended_2(advected_quantities, (("lat", 2),), 2, False)
    top_rows = advected_quantities[:, :, height - 2 :, :][:, :, ::-1, :]
    gathered = lax.all_gather(top_rows, "lon", axis=3, tiled=True)
    north_rows = jnp.take(gathered, opposite_counterpart, axis=3)
    across = attach(across, north_rows, is_top, 2)
    east_one = along[..., 3:-1]
    west_one = along[..., 1:-3]
    east_two = along[..., 4:]
    west_two = along[..., :-4]
    north_one = across[..., 3:-1, :]
    south_one = across[..., 1:-3, :]
    north_two = across[..., 4:, :]
    south_two = across[..., :-4, :]
    grad_east = (8.0 * (east_one - west_one) - (east_two - west_two)) / 12.0
    grad_north = (8.0 * (north_one - south_one) - (north_two - south_two)) / 12.0
    laplace = east_one + west_one + north_one + south_one - 4.0 * advected_quantities
    tendency = (
        -TIME_STEP * (easterly_speed * grad_east + poleward_speed * grad_north) + MIXING * laplace
    )
    updated = advected_quantities + wetness * tendency
    press_east = pressure(along[0][..., 1:-1], along[1][..., 1:-1], stratum_spans)
    press_north = pressure(across[0][:, 1:-1, :], across[1][:, 1:-1, :], stratum_spans)
    slope_east = 0.5 * (press_east[..., 2:] - press_east[..., :-2])
    slope_north = 0.5 * (press_north[:, 2:, :] - press_north[:, :-2, :])
    new_zonal = wetness * (easterly_speed - TIME_STEP * slope_east)
    new_meridional = wetness * (poleward_speed - TIME_STEP * slope_north)
    weights = stratum_spans[:, None, None]
    transports = jnp.stack(
        [jnp.sum(weights * new_zonal, axis=0), jnp.sum(weights * new_meridional, axis=0)]
    )
    flow_along = extended_2(transports, (("lon", 2),), 1, True)
    flow_across = extended_2(transports, (("lat", 1),), 1, False)
    top_flow = transports[:, height - 1 :, :]
    gathered_flow = lax.all_gather(top_flow, "lon", axis=2, tiled=True)
    flow_north = jnp.take(gathered_flow, opposite_counterpart, axis=2)
    flow_across = attach(flow_across, -flow_north, is_top, 1)
    divergence = 0.5 * (
        flow_along[0][:, 2:]
        - flow_along[0][:, :-2]
        + flow_across[1][2:, :]
        - flow_across[1][:-2, :]
    )
    right_side = wetness * (elevation_weights * elevation_anomaly - divergence)
    diagonal = 4.0 + elevation_weights
    solution = jnp.zeros_like(right_side)
    residual = right_side
    precond = residual / diagonal
    direction = precond
    norm_now = norm_sum(residual, precond)
    for step in range(ITERS):
        image = operate(direction, diagonal, wetness, opposite_counterpart, is_top)
        alpha = norm_now / lax.psum(jnp.sum(direction * image), ("lon", "lat"))
        solution = solution + alpha * direction
        residual = residual - alpha * image
        if step + 1 < ITERS:
            precond = residual / diagonal
            norm_next = norm_sum(residual, precond)
            direction = precond + norm_next / norm_now * direction
            norm_now = norm_next
    return (updated[0], updated[1], new_zonal, new_meridional, solution)


def solution(mesh):
    placed = (
        P(None, "lat", "lon"),
        P(None, "lat", "lon"),
        P(None, "lat", "lon"),
        P(None, "lat", "lon"),
        P(),
        P("lat", "lon"),
        P("lon"),
        P("lat", "lon"),
        P("lat", "lon"),
    )
    return jax.shard_map(
        body,
        mesh=mesh,
        in_specs=placed,
        out_specs=(
            P(None, "lat", "lon"),
            P(None, "lat", "lon"),
            P(None, "lat", "lon"),
            P(None, "lat", "lon"),
            P("lat", "lon"),
        ),
        check_vma=False,
    )
```

profile of v0, /device:TPU:1, one launch (start us, length us, event | category | flops | bytes accessed | tf_op | source)
XLA Modules:
  0.0 704.6 jit_solution(5909233039430501097)
XLA Ops:
  2.3 5.1 collective-permute-start.2
  7.5 1.9 collective-permute-start.3
  9.4 1.7 fusion.4
  11.4 7.3 %collective-permute-start = (f32[2,10,64,2]{2,3,1,0:T(2,128)S(1)}, f32[2,10,64,2]{2,3,1,0:T(2,128)S(1)}, u32[]{:S(2)}, u32[]{:S(2)}) collective-permute-start(f32[2,10,64,2]{2,3,1,0:T(2,128)S(1)} %copy.171), channel_id=1, source_target_pairs={{8,0},{16,8},{24,16},{32,24},{40,32},{48,40},{56,48},{64,56},{72,6... | collective-permute-start | bytes 30728 | tf_op jit(solution)/shard_map/ppermute | solution.py:27
  19.1 36.5 %all_gather.15 = f32[2,10,2,4096]{3,2,1,0:T(2,128)S(1)} all-gather(f32[2,10,2,128]{3,2,1,0:T(2,128)S(1)} %rev.3), channel_id=1, replica_groups=mesh['lon'=32,'lat'=8] {'lon'}, dimensions={3}, use_global_device_ids=true | all-gather | bytes 675840 | tf_op jit(solution)/shard_map/all_gather | solution.py:87
  55.7 8.1 %copy.155 = f32[2,10,2,4096]{1,2,3,0:T(2,128)} copy(f32[2,10,2,4096]{3,2,1,0:T(2,128)S(1)} %all_gather.15) | data formatting | bytes 1310720 | tf_op jit(solution)/shard_map/all_gather | solution.py:87
  63.8 5.1 gather_fusion
  70.7 1.6 reduce-window_subtract_fusion
  72.3 1.5 pad_maximum_fusion
  73.9 1.2 bitcast_select_fusion
  76.6 1.2 multiply_reduce_fusion
  79.6 3.7 collective-permute-start.5
  84.8 11.8 %collective-permute-start.6 = (f32[2,1,128]{0,2,1:T(8,128)}, f32[2,1,128]{0,2,1:T(8,128)}, u32[]{:S(2)}, u32[]{:S(2)}) collective-permute-start(f32[2,1,128]{0,2,1:T(8,128)} %copy.166), channel_id=1, source_target_pairs={{1,0},{2,1},{3,2},{4,3},{5,4},{6,5},{7,6},{9,8},{10,9},{11,10},{12... | collective-permute-start | bytes 3080 | tf_op jit(solution)/shard_map/ppermute | solution.py:27
  96.6 3.1 collective-permute-start.7
  100.6 43.3 %all_gather.16 = f32[2,1,4096]{0,2,1:T(8,128)} all-gather(f32[2,1,128]{0,2,1:T(8,128)} %copy.173), channel_id=1, replica_groups=mesh['lon'=32,'lat'=8] {'lon'}, dimensions={2}, use_global_device_ids=true | all-gather | bytes 33792 | tf_op jit(solution)/shard_map/all_gather | solution.py:118
  143.9 2.8 gather_fusion.1
  146.7 1.5 fusion.51
  148.2 1.6 fusion.53
  151.7 1.6 add_divide_fusion.2
  154.6 13.0 %collective-permute-start.10 = (f32[1,128]{1,0:T(1,128)}, f32[1,128]{1,0:T(1,128)}, u32[]{:S(2)}, u32[]{:S(2)}) collective-permute-start(f32[1,128]{1,0:T(1,128)} %get-tuple-element.66), channel_id=1, source_target_pairs={{1,0},{2,1},{3,2},{4,3},{5,4},{6,5},{7,6},{9,8},{10,9},{11,10},{12... | collective-permute-start | bytes 1544 | tf_op jit(solution)/shard_map/ppermute | solution.py:27
  167.5 28.0 %all_gather.17 = f32[1,4096]{1,0:T(1,128)S(1)} all-gather(f32[1,128]{1,0:T(1,128)} %get-tuple-element.67), channel_id=1, replica_groups=mesh['lon'=32,'lat'=8] {'lon'}, dimensions={1}, use_global_device_ids=true | all-gather | bytes 16896 | tf_op jit(solution)/shard_map/all_gather | solution.py:58
  195.6 11.0 %collective-permute-start.11 = (f32[1,128]{1,0:T(1,128)}, f32[1,128]{1,0:T(1,128)}, u32[]{:S(2)}, u32[]{:S(2)}) collective-permute-start(f32[1,128]{1,0:T(1,128)} %get-tuple-element.67), channel_id=1, source_target_pairs={{0,1},{1,2},{2,3},{3,4},{4,5},{5,6},{6,7},{8,9},{9,10},{10,11},{11... | collective-permute-start | bytes 1544 | tf_op jit(solution)/shard_map/ppermute | solution.py:25
  206.5 2.0 collective-permute-start.8
  208.6 1.9 gather_fusion.2
  211.1 3.8 collective-permute-done.9
  215.0 1.5 multiply_reduce_fusion.5
  216.5 74.7 %all-reduce = (f32[]{:T(128)}, f32[]{:T(128)}) all-reduce(f32[]{:T(128)} %get-tuple-element.22, f32[]{:T(128)} %get-tuple-element.21), channel_id=1, replica_groups=mesh['lon'=32,'lat'=8] {'lon','lat'}, use_global_device_ids=true, to_apply=%region_5.6 | all-reduce | flops 2 | bytes 16 | tf_op jit(solution)/shard_map/psum | solution.py:66
  292.6 2.0 multiply_reduce_fusion.4
  294.6 73.5 %psum.44 = f32[]{:T(128)} all-reduce(f32[]{:T(128)} %get-tuple-element.29), channel_id=1, replica_groups=mesh['lon'=32,'lat'=8] {'lon','lat'}, use_global_device_ids=true, to_apply=%region_9.11 | all-reduce | flops 1 | bytes 8 | tf_op jit(solution)/shard_map/psum | solution.py:66
  371.4 2.6 collective-permute-start.14
  374.0 27.8 %all_gather.18 = f32[1,4096]{1,0:T(1,128)S(1)} all-gather(f32[1,128]{1,0:T(1,128)} %get-tuple-element.63), channel_id=1, replica_groups=mesh['lon'=32,'lat'=8] {'lon'}, dimensions={1}, use_global_device_ids=true | all-gather | bytes 16896 | tf_op jit(solution)/shard_map/all_gather | solution.py:58
  401.7 11.9 %collective-permute-start.15 = (f32[1,128]{1,0:T(1,128)}, f32[1,128]{1,0:T(1,128)}, u32[]{:S(2)}, u32[]{:S(2)}) collective-permute-start(f32[1,128]{1,0:T(1,128)} %get-tuple-element.63), channel_id=1, source_target_pairs={{0,1},{1,2},{2,3},{3,4},{4,5},{5,6},{6,7},{8,9},{9,10},{10,11},{11... | collective-permute-start | bytes 1544 | tf_op jit(solution)/shard_map/ppermute | solution.py:25
  413.7 1.5 collective-permute-start.12
  415.2 1.8 gather_fusion.3
  417.7 3.9 collective-permute-done.13
  421.6 2.1 multiply_reduce_fusion.3
  423.7 72.7 %psum.45 = f32[]{:T(128)} all-reduce(f32[]{:T(128)} %get-tuple-element.27), channel_id=1, replica_groups=mesh['lon'=32,'lat'=8] {'lon','lat'}, use_global_device_ids=true, to_apply=%region_11.13 | all-reduce | flops 1 | bytes 8 | tf_op jit(solution)/shard_map/psum | solution.py:136
  497.5 1.4 multiply_reduce_fusion.2
  498.9 3.2 fusion.12
  502.1 73.6 %psum.46 = f32[]{:T(128)} all-reduce(f32[]{:T(128)} %multiply_reduce_fusion.2), channel_id=1, replica_groups=mesh['lon'=32,'lat'=8] {'lon','lat'}, use_global_device_ids=true, to_apply=%region_13.15 | all-reduce | flops 1 | bytes 8 | tf_op jit(solution)/shard_map/psum | solution.py:66
  577.8 2.6 collective-permute-start.18
  580.4 28.4 %all_gather.19 = f32[1,4096]{1,0:T(1,128)S(1)} all-gather(f32[1,128]{1,0:T(1,128)S(1)} %get-tuple-element.59), channel_id=1, replica_groups=mesh['lon'=32,'lat'=8] {'lon'}, dimensions={1}, use_global_device_ids=true | all-gather | bytes 16896 | tf_op jit(solution)/shard_map/all_gather | solution.py:58
  608.8 11.4 %collective-permute-start.19 = (f32[1,128]{1,0:T(1,128)S(1)}, f32[1,128]{1,0:T(1,128)S(1)}, u32[]{:S(2)}, u32[]{:S(2)}) collective-permute-start(f32[1,128]{1,0:T(1,128)S(1)} %get-tuple-element.59), channel_id=1, source_target_pairs={{0,1},{1,2},{2,3},{3,4},{4,5},{5,6},{6,7},{8,9},{9,10},{10,11},{11... | collective-permute-start | bytes 1544 | tf_op jit(solution)/shard_map/ppermute | solution.py:25
  620.2 1.5 collective-permute-start.16
  621.8 1.3 gather_fusion.4
  623.1 4.7 collective-permute-done.17
  627.8 1.4 fusion.58
  630.1 72.6 %psum.47 = f32[]{:T(128)} all-reduce(f32[]{:T(128)} %fusion.58), channel_id=1, replica_groups=mesh['lon'=32,'lat'=8] {'lon','lat'}, use_global_device_ids=true, to_apply=%region_15.17 | all-reduce | flops 1 | bytes 8 | tf_op jit(solution)/shard_map/psum | solution.py:136
  (99 shorter events, 18.8 us)
Async XLA Ops:
  2.3 71.5 %collective-permute-start.2 = (f32[2,10,2,128]{1,2,0,3:T(2,128)}, f32[2,10,2,128]{1,2,0,3:T(2,128)}, u32[]{:S(2)}, u32[]{:S(2)}) collective-permute-start(f32[2,10,2,128]{1,2,0,3:T(2,128)} %copy.156), channel_id=1, source_target_pairs={{1,0},{2,1},{3,2},{4,3},{5,4},{6,5},{7,6},{9,8},{10,9},{11,10},{12... | collective-permute-start | bytes 61448 | tf_op jit(solution)/shard_map/ppermute | solution.py:27
  7.5 11.6 %copy-start.18 = (s32[128]{0:T(128)S(1)}, s32[128]{0:T(128)}, u32[]{:S(2)}) copy-start(s32[128]{0:T(128)} %param.17) | copy-start | bytes 1540
  7.5 67.7 %collective-permute-start.3 = (f32[2,10,2,128]{3,2,1,0:T(2,128)S(1)}, f32[2,10,2,128]{3,2,1,0:T(2,128)S(1)}, u32[]{:S(2)}, u32[]{:S(2)}) collective-permute-start(f32[2,10,2,128]{3,2,1,0:T(2,128)S(1)} %get-tuple-element.49), channel_id=1, source_target_pairs={{0,1},{1,2},{2,3},{3,4},{4,5},{5,6},{6,7},{8,9},{9,10},{10,11},{11... | collective-permute-start | bytes 61448 | tf_op jit(solution)/shard_map/ppermute | solution.py:25
  11.4 57.5 %collective-permute-start = (f32[2,10,64,2]{2,3,1,0:T(2,128)S(1)}, f32[2,10,64,2]{2,3,1,0:T(2,128)S(1)}, u32[]{:S(2)}, u32[]{:S(2)}) collective-permute-start(f32[2,10,64,2]{2,3,1,0:T(2,128)S(1)} %copy.171), channel_id=1, source_target_pairs={{8,0},{16,8},{24,16},{32,24},{40,32},{48,40},{56,48},{64,56},{72,6... | collective-permute-start | bytes 30728 | tf_op jit(solution)/shard_map/ppermute | solution.py:27
  18.9 50.2 %collective-permute-start.1 = (f32[2,10,64,2]{2,3,1,0:T(2,128)S(1)}, f32[2,10,64,2]{2,3,1,0:T(2,128)S(1)}, u32[]{:S(2)}, u32[]{:S(2)}) collective-permute-start(f32[2,10,64,2]{2,3,1,0:T(2,128)S(1)} %copy.172), channel_id=1, source_target_pairs={{0,8},{8,16},{16,24},{24,32},{32,40},{40,48},{48,56},{56,64},{64,7... | collective-permute-start | bytes 30728 | tf_op jit(solution)/shard_map/ppermute | solution.py:25
  55.6 88.3 %copy-start.17 = (s32[1024]{0:T(1024)}, s32[1024]{0:T(1024)S(1)}, u32[]{:S(2)}) copy-start(s32[1024]{0:T(1024)S(1)} %pad_clamp_fusion) | copy-start | bytes 12292
  55.6 8.2 %copy-start.6 = (s32[64,128]{1,0:T(8,128)S(1)}, s32[64,128]{1,0:T(8,128)}, u32[]{:S(2)}) copy-start(s32[64,128]{1,0:T(8,128)} %param.16) | copy-start | bytes 98308
  63.8 5.7 copy-start
  63.8 5.7 copy-start.1
  63.8 12.3 %copy-start.12 = (f32[64,128]{1,0:T(8,128)}, f32[64,128]{1,0:T(8,128)S(1)}, u32[]{:S(2)}) copy-start(f32[64,128]{1,0:T(8,128)S(1)} %convert_element_type.3) | copy-start | bytes 98308
  70.1 0.7 copy-start.16
  72.3 1.5 copy-start.11
  75.2 0.6 copy-start.13
  75.2 0.6 copy-start.14
  75.3 1.1 copy-start.4
  75.3 1.2 copy-start.9
  75.3 1.2 copy-start.10
  77.8 68.9 %copy-start.5 = (f32[64,128]{1,0:T(8,128)}, f32[64,128]{1,0:T(8,128)S(1)}, u32[]{:S(2)}) copy-start(f32[64,128]{1,0:T(8,128)S(1)} %get-tuple-element.24) | copy-start | bytes 98308
  78.5 68.2 %collective-permute-start.4 = (f32[2,64,1]{2,1,0:T(8,128)}, f32[2,64,1]{2,1,0:T(8,128)}, u32[]{:S(2)}, u32[]{:S(2)}) collective-permute-start(f32[2,64,1]{2,1,0:T(8,128)} %get-tuple-element.52), channel_id=1, source_target_pairs={{0,8},{8,16},{16,24},{24,32},{32,40},{40,48},{48,56},{56,64},{64,7... | collective-permute-start | bytes 1544 | tf_op jit(solution)/shard_map/ppermute | solution.py:25
  79.6 67.1 %collective-permute-start.5 = (f32[2,64,1]{2,1,0:T(8,128)}, f32[2,64,1]{2,1,0:T(8,128)}, u32[]{:S(2)}, u32[]{:S(2)}) collective-permute-start(f32[2,64,1]{2,1,0:T(8,128)} %get-tuple-element.53), channel_id=1, source_target_pairs={{8,0},{16,8},{24,16},{32,24},{40,32},{48,40},{56,48},{64,56},{72,6... | collective-permute-start | bytes 1544 | tf_op jit(solution)/shard_map/ppermute | solution.py:27
  84.8 63.4 %collective-permute-start.6 = (f32[2,1,128]{0,2,1:T(8,128)}, f32[2,1,128]{0,2,1:T(8,128)}, u32[]{:S(2)}, u32[]{:S(2)}) collective-permute-start(f32[2,1,128]{0,2,1:T(8,128)} %copy.166), channel_id=1, source_target_pairs={{1,0},{2,1},{3,2},{4,3},{5,4},{6,5},{7,6},{9,8},{10,9},{11,10},{12... | collective-permute-start | bytes 3080 | tf_op jit(solution)/shard_map/ppermute | solution.py:27
  96.6 54.1 %collective-permute-start.7 = (f32[2,1,128]{0,2,1:T(8,128)}, f32[2,1,128]{0,2,1:T(8,128)}, u32[]{:S(2)}, u32[]{:S(2)}) collective-permute-start(f32[2,1,128]{0,2,1:T(8,128)} %copy.173), channel_id=1, source_target_pairs={{0,1},{1,2},{2,3},{3,4},{4,5},{5,6},{6,7},{8,9},{9,10},{10,11},{11... | collective-permute-start | bytes 3080 | tf_op jit(solution)/shard_map/ppermute | solution.py:25
  100.5 51.1 %copy-start.2 = (f32[64,128]{1,0:T(8,128)S(1)}, f32[64,128]{1,0:T(8,128)}, u32[]{:S(2)}) copy-start(f32[64,128]{1,0:T(8,128)} %param.18) | copy-start | bytes 98308
  154.6 55.9 %collective-permute-start.10 = (f32[1,128]{1,0:T(1,128)}, f32[1,128]{1,0:T(1,128)}, u32[]{:S(2)}, u32[]{:S(2)}) collective-permute-start(f32[1,128]{1,0:T(1,128)} %get-tuple-element.66), channel_id=1, source_target_pairs={{1,0},{2,1},{3,2},{4,3},{5,4},{6,5},{7,6},{9,8},{10,9},{11,10},{12... | collective-permute-start | bytes 1544 | tf_op jit(solution)/shard_map/ppermute | solution.py:27
  195.6 19.4 %collective-permute-start.11 = (f32[1,128]{1,0:T(1,128)}, f32[1,128]{1,0:T(1,128)}, u32[]{:S(2)}, u32[]{:S(2)}) collective-permute-start(f32[1,128]{1,0:T(1,128)} %get-tuple-element.67), channel_id=1, source_target_pairs={{0,1},{1,2},{2,3},{3,4},{4,5},{5,6},{6,7},{8,9},{9,10},{10,11},{11... | collective-permute-start | bytes 1544 | tf_op jit(solution)/shard_map/ppermute | solution.py:25
  206.5 4.6 collective-permute-start.8
  208.6 6.4 collective-permute-start.9
  211.1 3.8 copy-start.15
  371.4 45.6 %collective-permute-start.14 = (f32[1,128]{1,0:T(1,128)}, f32[1,128]{1,0:T(1,128)}, u32[]{:S(2)}, u32[]{:S(2)}) collective-permute-start(f32[1,128]{1,0:T(1,128)} %get-tuple-element.62), channel_id=1, source_target_pairs={{1,0},{2,1},{3,2},{4,3},{5,4},{6,5},{7,6},{9,8},{10,9},{11,10},{12... | collective-permute-start | bytes 1544 | tf_op jit(solution)/shard_map/ppermute | solution.py:27
  401.7 19.8 %collective-permute-start.15 = (f32[1,128]{1,0:T(1,128)}, f32[1,128]{1,0:T(1,128)}, u32[]{:S(2)}, u32[]{:S(2)}) collective-permute-start(f32[1,128]{1,0:T(1,128)} %get-tuple-element.63), channel_id=1, source_target_pairs={{0,1},{1,2},{2,3},{3,4},{4,5},{5,6},{6,7},{8,9},{9,10},{10,11},{11... | collective-permute-start | bytes 1544 | tf_op jit(solution)/shard_map/ppermute | solution.py:25
  413.7 4.0 collective-permute-start.12
  415.2 6.4 collective-permute-start.13
  498.9 124.1 %copy-start.19 = (s32[128]{0:T(128)S(1)}, s32[128]{0:T(128)}, u32[]{:S(2)}) copy-start(s32[128]{0:T(128)} %param.17) | copy-start | bytes 1540
  502.1 127.1 %copy-start.3 = (f32[2,10,64,128]{3,2,1,0:T(8,128)S(1)}, f32[2,10,64,128]{3,2,1,0:T(8,128)}, u32[]{:S(2)}) copy-start(f32[2,10,64,128]{3,2,1,0:T(8,128)} %fusion.12) | copy-start | bytes 1966084
  502.1 201.8 %copy-start.7 = (f32[64,128]{1,0:T(8,128)S(1)}, f32[64,128]{1,0:T(8,128)}, u32[]{:S(2)}) copy-start(f32[64,128]{1,0:T(8,128)} %get-tuple-element.30) | copy-start | bytes 98308
  502.1 201.8 %copy-start.8 = (f32[64,128]{1,0:T(8,128)S(1)}, f32[64,128]{1,0:T(8,128)}, u32[]{:S(2)}) copy-start(f32[64,128]{1,0:T(8,128)} %get-tuple-element.28) | copy-start | bytes 98308
  577.8 45.2 %collective-permute-start.18 = (f32[1,128]{1,0:T(1,128)S(1)}, f32[1,128]{1,0:T(1,128)S(1)}, u32[]{:S(2)}, u32[]{:S(2)}) collective-permute-start(f32[1,128]{1,0:T(1,128)S(1)} %get-tuple-element.58), channel_id=1, source_target_pairs={{1,0},{2,1},{3,2},{4,3},{5,4},{6,5},{7,6},{9,8},{10,9},{11,10},{12... | collective-permute-start | bytes 1544 | tf_op jit(solution)/shard_map/ppermute | solution.py:27
  608.8 19.1 %collective-permute-start.19 = (f32[1,128]{1,0:T(1,128)S(1)}, f32[1,128]{1,0:T(1,128)S(1)}, u32[]{:S(2)}, u32[]{:S(2)}) collective-permute-start(f32[1,128]{1,0:T(1,128)S(1)} %get-tuple-element.59), channel_id=1, source_target_pairs={{0,1},{1,2},{2,3},{3,4},{4,5},{5,6},{6,7},{8,9},{9,10},{10,11},{11... | collective-permute-start | bytes 1544 | tf_op jit(solution)/shard_map/ppermute | solution.py:25
  620.2 2.9 collective-permute-start.16
  621.7 6.1 collective-permute-start.17
where the time goes:
time: 707 us; the launch traced here: 705 us
  blocking collectives  531 us (75%)
  starting transfers between devices  91.6 us (13%)
  local copies, waits for them, and re-layouts  31.6 us (4%)
  other arithmetic  30.7 us (4%)
  waiting for transfers between devices  12.5 us (2%)
  between operations  7.26 us (1%)
    psum x3, blocking collectives, norm_sum(): return lax.psum(jnp.sum(residual * precond), ('lon', 'lat'))  222 us
    psum x2, blocking collectives, body(): alpha = norm_now / lax.psum(jnp.sum(direction * image), ('lon', 'lat'))  145 us
    all_gather x3, blocking collectives, operate(): gathered = lax.all_gather(field[height - 1:, :], 'lon', axis=1, tiled=True)  84.2 us
    ppermute x10, starting transfers between devices, extended_2(): lax.ppermute(head, axis, [((i + 1) % count, i) for i in range(ends)])  51.1 us
    all_gather x1, blocking collectives, body(): gathered_flow = lax.all_gather(top_flow, 'lon', axis=2, tiled=True)  43.3 us
    ppermute x10, starting transfers between devices, extended_2(): lax.ppermute(tail, axis, [(i, (i + 1) % count) for i in range(ends)])  40.5 us
    all_gather x1, blocking collectives, body(): gathered = lax.all_gather(top_rows, 'lon', axis=3, tiled=True)  36.5 us
  transfers between devices with their start and end apart: 20, of which 3 were waited for; matrix products, arithmetic and copies ran while one was open for 5% of the time, Pallas kernels for 0%

commit v1 on v0

v1 whole, which is shorter than its diff:
```python
import functools

import jax
import jax.numpy as jnp
from jax import lax
from jax.experimental import pallas as pl
from jax.experimental.pallas import tpu as pltpu
from jax.sharding import PartitionSpec as P

MESH = pl.DeviceIdType.MESH
LEVELS = 10
ROWS = 64
LANES = 128
EDGE = 8
NLON = 32
NLAT = 8
NX = 4
NZ = 8
SPAN2 = 10
SPAN3 = 4
FOLD2 = 20
FOLD3 = 4 * LEVELS


def density(t, s):
    return -t - 0.15 * t * t + 0.8 * s - 0.2 * t * s


def lane_iota(rows):
    return lax.broadcasted_iota(jnp.int32, (rows, LANES), 1)


def kernel(
    t_hbm, s_hbm, u_hbm, v_hbm, w_hbm, e_hbm, a_hbm, spans, opp,
    nt, ns, nu, nv, surf,
    ts, uv, wbuf, ebuf, x, pack, wide, pack3, wide3, own2, fold2, own3, fold3, press, vec, sums1, sums2,
    in_sem, side_send, side_recv, group_send, group_recv,
):
    lon = lax.axis_index("lon")
    lat = lax.axis_index("lat")
    lon_x = lax.rem(lon, NX)
    east = lax.rem(lon + 1, NLON)
    west = lax.rem(lon + NLON - 1, NLON)
    is_top = lat == NLAT - 1
    is_low = lat == 0
    not_top = lat < NLAT - 1
    not_low = lat > 0

    loads = [
        pltpu.make_async_copy(w_hbm, wbuf, in_sem.at[0]),
        pltpu.make_async_copy(e_hbm, ebuf.at[0], in_sem.at[1]),
        pltpu.make_async_copy(a_hbm, ebuf.at[1], in_sem.at[2]),
        pltpu.make_async_copy(t_hbm, ts.at[0, :, EDGE:EDGE + ROWS, :], in_sem.at[3]),
        pltpu.make_async_copy(s_hbm, ts.at[1, :, EDGE:EDGE + ROWS, :], in_sem.at[4]),
        pltpu.make_async_copy(u_hbm, uv.at[0], in_sem.at[5]),
        pltpu.make_async_copy(v_hbm, uv.at[1], in_sem.at[6]),
    ]
    for load in loads:
        load.start()

    barrier = pltpu.get_barrier_semaphore()

    def greet(dev):
        pl.semaphore_signal(barrier, inc=1, device_id=dev, device_id_type=MESH)

    near = []
    for dx in range(NX):
        for dy in range(NLAT):
            if dx or dy:
                near.append((lon - lon_x + lax.rem(lon_x + dx, NX), lax.rem(lat + dy, NLAT)))
    far = [(lax.rem(lon + NX * k, NLON), lat) for k in range(1, NZ)]
    ring = [(lax.rem(lon + k, NLON), lat) for k in range(1, NLON)]
    for dev in near + far + [(east, lat), (west, lat)]:
        greet(dev)

    @pl.when(not_top)
    def _():
        greet((east, lat + 1))
        greet((west, lat + 1))

    @pl.when(not_low)
    def _():
        greet((east, lat - 1))
        greet((west, lat - 1))

    @pl.when(is_top)
    def _():
        for dev in ring:
            greet(dev)

    for load in loads[:3]:
        load.wait()
    own = slice(EDGE, EDGE + ROWS)
    weights = ebuf[0]
    diagonal = 4.0 + weights
    wetness = wbuf[...].astype(jnp.float32)
    scale = wetness / diagonal
    x[3, 0, own, :] = scale
    x[4, 0, own, :] = scale * (weights * ebuf[1])

    for load in loads[3:]:
        load.wait()
    zero = jnp.zeros((ROWS, LANES), jnp.float32)
    below, press_sum, east_sum, north_sum = zero, zero, zero, zero
    for k in range(LEVELS):
        span = spans[k]
        layer = density(ts[0, k, own, :], ts[1, k, own, :]) * span
        press_sum = press_sum + span * (below + 0.5 * layer)
        below = below + layer
        east_sum = east_sum + span * uv[0, k]
        north_sum = north_sum + span * uv[1, k]
    x[0, 0, own, :] = press_sum
    x[1, 0, own, :] = east_sum
    x[2, 0, own, :] = north_sum

    lanes = lane_iota(ROWS)
    packed = zero
    for f in range(5):
        moved = pltpu.roll(x[f, 0, own, :], SPAN2 * f + 5, 1)
        packed = jnp.where((lanes >= SPAN2 * f) & (lanes < SPAN2 * (f + 1)), moved, packed)
    pack[...] = packed
    packed = zero
    for q in range(2 * LEVELS):
        moved = pltpu.roll(ts[q // LEVELS, q % LEVELS, own, :], SPAN3 * q + 2, 1)
        packed = jnp.where((lanes >= SPAN3 * q) & (lanes < SPAN3 * (q + 1)), moved, packed)
    pack3[...] = packed

    @pl.when(is_top)
    def _():
        row = 0
        for f, count in ((0, 5), (1, 3), (2, 4), (3, 4), (4, 4)):
            for r in range(count):
                last = EDGE + ROWS - 1 - r
                line = x[f, 0, last:last + 1, :]
                own2[row:row + 1, :] = -line if f in (1, 2) else line
                row += 1
        fold2[lon, 0:FOLD2, :] = own2[0:FOLD2, :]
        for q in range(2 * LEVELS):
            own3[2 * q:2 * q + 2, :] = ts[q // LEVELS, q % LEVELS, EDGE + ROWS - 2:EDGE + ROWS, :]
        fold3[lon] = own3[...]
        for f in range(5):
            x[f, 0, EDGE + ROWS:, :] = jnp.zeros((EDGE, LANES), jnp.float32)

    @pl.when(is_low)
    def _():
        for f in range(5):
            x[f, 0, 0:EDGE, :] = jnp.zeros((EDGE, LANES), jnp.float32)
        for q in range(2 * LEVELS):
            ts[q // LEVELS, q % LEVELS, 0:EDGE, :] = jnp.zeros((EDGE, LANES), jnp.float32)

    base = 31 + 7 + 2

    @pl.when(is_top)
    def _():
        pl.semaphore_wait(barrier, base + 2 + NLON - 1)

    @pl.when(is_low)
    def _():
        pl.semaphore_wait(barrier, base + 2)

    @pl.when(not_top & not_low)
    def _():
        pl.semaphore_wait(barrier, base + 4)

    def copy(src, dst, sem, dev):
        return pltpu.make_async_remote_copy(
            src_ref=src, dst_ref=dst, send_sem=side_send.at[sem], recv_sem=side_recv.at[sem],
            device_id=dev, device_id_type=MESH,
        )

    top_rows = slice(EDGE + ROWS, EDGE + ROWS + EDGE)
    to_east = copy(pack, wide.at[0, own, :], 0, (east, lat))
    to_west = copy(pack, wide.at[1, own, :], 1, (west, lat))
    to_north = copy(x.at[:, 0, ROWS:EDGE + ROWS, :], x.at[:, 0, 0:EDGE, :], 2, (lon, lat + 1))
    to_ne = copy(pack.at[ROWS - EDGE:ROWS, :], wide.at[0, 0:EDGE, :], 3, (east, lat + 1))
    to_nw = copy(pack.at[ROWS - EDGE:ROWS, :], wide.at[1, 0:EDGE, :], 4, (west, lat + 1))
    to_south = copy(x.at[:, 0, EDGE:2 * EDGE, :], x.at[:, 0, top_rows, :], 5, (lon, lat - 1))
    to_se = copy(pack.at[0:EDGE, :], wide.at[0, top_rows, :], 6, (east, lat - 1))
    to_sw = copy(pack.at[0:EDGE, :], wide.at[1, top_rows, :], 7, (west, lat - 1))
    to_east3 = copy(pack3, wide3.at[0], 8, (east, lat))
    to_west3 = copy(pack3, wide3.at[1], 9, (west, lat))
    to_north3 = copy(
        ts.at[:, :, EDGE + ROWS - 2:EDGE + ROWS, :], ts.at[:, :, EDGE - 2:EDGE, :], 10, (lon, lat + 1)
    )
    to_south3 = copy(
        ts.at[:, :, EDGE:EDGE + 2, :], ts.at[:, :, EDGE + ROWS:EDGE + ROWS + 2, :], 11, (lon, lat - 1)
    )
    north_sends = (to_north, to_ne, to_nw)
    south_sends = (to_south, to_se, to_sw)

    def spread(src, dst, sem, devs):
        for dev in devs:
            pltpu.make_async_remote_copy(
                src_ref=src, dst_ref=dst, send_sem=group_send.at[sem], recv_sem=group_recv.at[sem],
                device_id=dev, device_id_type=MESH,
            ).start()

    def settle(ref, sem):
        pltpu.make_async_copy(ref, ref, sem).wait()

    @pl.when(is_top)
    def _():
        spread(own2.at[0:FOLD2, :], fold2.at[lon, 0:FOLD2, :], 0, ring)

    to_east.start()
    to_west.start()

    @pl.when(not_top)
    def _():
        for send in north_sends:
            send.start()

    @pl.when(not_low)
    def _():
        for send in south_sends:
            send.start()

    to_east3.start()
    to_west3.start()

    @pl.when(not_top)
    def _():
        to_north3.start()

    @pl.when(not_low)
    def _():
        to_south3.start()

    @pl.when(is_top)
    def _():
        spread(own3, fold3.at[lon], 1, ring)

    to_east.wait_recv()
    to_west.wait_recv()

    @pl.when(not_low)
    def _():
        for send in north_sends:
            send.wait_recv()

    @pl.when(not_top)
    def _():
        for send in south_sends:
            send.wait_recv()

    lanes_w = lane_iota(EDGE + ROWS + EDGE)
    eastern = lax.rem(lanes_w, SPAN2) < 5
    merged = jnp.where(eastern, wide[0], wide[1])
    for f in range(5):
        x[f, 1] = pltpu.roll(merged, LANES - (SPAN2 * f + 5), 1)

    @pl.when(is_low)
    def _():
        for f in range(5):
            x[f, 1, 0:EDGE, :] = jnp.zeros((EDGE, LANES), jnp.float32)

    lanes_e = lane_iota(EDGE)
    first = opp[0]
    slot = lax.div(first, LANES)
    offset = first - slot * LANES
    slot_p = lax.rem(slot + 1, NLON)
    slot_m = lax.rem(slot + NLON - 1, NLON)
    slot_mm = lax.rem(slot + NLON - 2, NLON)
    index = (offset - lanes_e) & (LANES - 1)

    def turn(tile):
        return jnp.take_along_axis(tile, index, axis=1)

    @pl.when(is_top)
    def _():
        settle(fold2.at[0:NLON - 1, 0:FOLD2, :], group_recv.at[0])
        kept = lanes_e <= offset
        near_half = index < LANES // 2
        mine, aside = [], []
        for tile in range(3):
            part = slice(EDGE * tile, EDGE * (tile + 1))
            b_p, b_0, b_m, b_mm = (fold2[s, part, :] for s in (slot_p, slot, slot_m, slot_mm))
            mine.append(turn(jnp.where(kept, b_0, b_m)))
            right = jnp.where(kept, b_m, b_mm)
            left = jnp.where(kept, b_p, b_0)
            aside.append(turn(jnp.where(near_half, right, left)))
        for half, tiles in ((0, mine), (1, aside)):
            x[0, half, EDGE + ROWS:EDGE + ROWS + 5, :] = tiles[0][0:5]
            x[1, half, EDGE + ROWS:EDGE + ROWS + 3, :] = tiles[0][5:8]
            x[2, half, EDGE + ROWS:EDGE + ROWS + 4, :] = tiles[1][0:4]
            x[3, half, EDGE + ROWS:EDGE + ROWS + 4, :] = tiles[1][4:8]
            x[4, half, EDGE + ROWS:EDGE + ROWS + 4, :] = tiles[2][0:4]

    full = EDGE + ROWS + EDGE
    first_lane = lanes_w == 0
    last_lane = lanes_w == LANES - 1

    def plus_east(a, b):
        return (
            pltpu.roll(jnp.where(first_lane, b, a), LANES - 1, 1),
            pltpu.roll(jnp.where(first_lane, a, b), LANES - 1, 1),
        )

    def plus_west(a, b):
        return (
            pltpu.roll(jnp.where(last_lane, b, a), 1, 1),
            pltpu.roll(jnp.where(last_lane, a, b), 1, 1),
        )

    def north_of(a):
        return pltpu.roll(a, full - 1, 0)

    def south_of(a):
        return pltpu.roll(a, 1, 0)

    scale2 = (x[3, 0], x[3, 1])
    wet2 = (scale2[0] > 0.0, scale2[1] > 0.0)
    q2 = (x[0, 0], x[0, 1])
    q_e = plus_east(*q2)
    q_w = plus_west(*q2)
    flow_e, flow_n = [], []
    for h in range(2):
        flow_e.append(jnp.where(wet2[h], x[1, h] - 0.05 * (q_e[h] - q_w[h]), 0.0))
        flow_n.append(jnp.where(wet2[h], x[2, h] - 0.05 * (north_of(q2[h]) - south_of(q2[h])), 0.0))
    f_e = plus_east(*flow_e)
    f_w = plus_west(*flow_e)
    basis = []
    v = tuple(
        x[4, h] - scale2[h] * (0.5 * (f_e[h] - f_w[h] + north_of(flow_n[h]) - south_of(flow_n[h])))
        for h in range(2)
    )
    basis.append(v[0][EDGE:EDGE + ROWS])
    for _ in range(3):
        v_e = plus_east(*v)
        v_w = plus_west(*v)
        v = tuple(scale2[h] * (v_e[h] + v_w[h] + north_of(v[h]) + south_of(v[h])) for h in range(2))
        basis.append(v[0][EDGE:EDGE + ROWS])

    for i in range(3):
        press[i, own, :] = basis[i]
    sub = lax.broadcasted_iota(jnp.int32, (EDGE, LANES), 0)
    table = jnp.zeros((EDGE, LANES), jnp.float32)
    for j, (l, r) in enumerate(((0, 0), (0, 1), (1, 1), (1, 2), (2, 2), (2, 3))):
        product = (diagonal * basis[l]) * basis[r]
        line = jnp.sum(product.reshape(ROWS // EDGE, EDGE, LANES), axis=0)
        line = jnp.sum(line, axis=0, keepdims=True)
        table = jnp.where(sub == j, line, table)
    table = jnp.sum(table, axis=1, keepdims=True)
    message = jnp.sum(jnp.where(sub == lanes_e, table, 0.0), axis=0, keepdims=True)
    vec[0:1, :] = message
    mine1 = lon_x * NLAT + lat
    sums1[pl.ds(mine1, 1), :] = message
    spread(vec.at[0:1, :], sums1.at[pl.ds(mine1, 1), :], 2, near)

    to_east3.wait_recv()
    to_west3.wait_recv()

    @pl.when(not_low)
    def _():
        to_north3.wait_recv()

    @pl.when(not_top)
    def _():
        to_south3.wait_recv()

    @pl.when(is_top)
    def _():
        settle(fold3.at[0:NLON - 1], group_recv.at[1])
        kept = lanes_e <= offset
        for tile in range(FOLD3 // EDGE):
            part = slice(EDGE * tile, EDGE * (tile + 1))
            turned = turn(jnp.where(kept, fold3[slot, part, :], fold3[slot_m, part, :]))
            for i in range(EDGE):
                q, r = (EDGE * tile + i) // 2, (EDGE * tile + i) % 2
                ts[q // LEVELS, q % LEVELS, EDGE + ROWS + 1 - r:EDGE + ROWS + 2 - r, :] = turned[i:i + 1]

    merged3 = jnp.where((lanes & 2) == 0, wide3[0], wide3[1])
    below = jnp.zeros((full, LANES), jnp.float32)
    below_side = zero
    tracer_out = (nt, ns)
    for k in range(LEVELS):
        span = spans[k]
        u = uv[0, k]
        w = uv[1, k]
        sides = []
        for f in range(2):
            side = pltpu.roll(merged3, LANES - (SPAN3 * (f * LEVELS + k) + 2), 1)
            sides.append(side)
            c = ts[f, k, EDGE:EDGE + ROWS, :]
            e1 = pltpu.roll(jnp.where(lanes == 0, side, c), LANES - 1, 1)
            e2 = pltpu.roll(jnp.where(lanes < 2, side, c), LANES - 2, 1)
            w1 = pltpu.roll(jnp.where(lanes == LANES - 1, side, c), 1, 1)
            w2 = pltpu.roll(jnp.where(lanes >= LANES - 2, side, c), 2, 1)
            n1 = ts[f, k, EDGE + 1:EDGE + ROWS + 1, :]
            n2 = ts[f, k, EDGE + 2:EDGE + ROWS + 2, :]
            s1 = ts[f, k, EDGE - 1:EDGE + ROWS - 1, :]
            s2 = ts[f, k, EDGE - 2:EDGE + ROWS - 2, :]
            grad_e = (8.0 * (e1 - w1) - (e2 - w2)) * (1.0 / 12.0)
            grad_n = (8.0 * (n1 - s1) - (n2 - s2)) * (1.0 / 12.0)
            laplace = e1 + w1 + n1 + s1 - 4.0 * c
            tracer_out[f][k] = c + wetness * (-0.1 * (u * grad_e + w * grad_n) + 0.1 * laplace)
        layer = density(ts[0, k], ts[1, k]) * span
        level = below + 0.5 * layer
        below = below + layer
        layer_side = density(sides[0], sides[1]) * span
        level_side = below_side + 0.5 * layer_side
        below_side = below_side + layer_side
        centre = level[EDGE:EDGE + ROWS]
        p_e = pltpu.roll(jnp.where(lanes == 0, level_side, centre), LANES - 1, 1)
        p_w = pltpu.roll(jnp.where(lanes == LANES - 1, level_side, centre), 1, 1)
        p_n = north_of(level)[EDGE:EDGE + ROWS]
        p_s = south_of(level)[EDGE:EDGE + ROWS]
        nu[k] = wetness * (u - 0.05 * (p_e - p_w))
        nv[k] = wetness * (w - 0.05 * (p_n - p_s))

    settle(sums1.at[0:NX * NLAT - 1, :], group_recv.at[2])
    total = jnp.sum(sums1[...], axis=0, keepdims=True)
    mine2 = lax.div(lon, NX)
    vec[EDGE:EDGE + 1, :] = total
    sums2[pl.ds(mine2, 1), :] = total
    spread(vec.at[EDGE:EDGE + 1, :], sums2.at[pl.ds(mine2, 1), :], 3, far)
    settle(sums2.at[0:NZ - 1, :], group_recv.at[3])
    total = jnp.sum(sums2[...], axis=0, keepdims=True)
    mu = [total[:, j:j + 1] for j in range(6)]

    def gram(a, b, shift):
        out = None
        for i, ai in enumerate(a):
            for j, bj in enumerate(b):
                term = ai * bj * mu[i + j + shift]
                out = term if out is None else out + term
        return out

    one = jnp.ones((1, 1), jnp.float32)
    res, dire, sol = [one], [one], [0.0 * one] * 3
    rz = mu[0]
    for step in range(3):
        alpha = rz / (gram(dire, dire, 0) - gram(dire, dire, 1))
        sol = [sol[i] + alpha * dire[i] if i < len(dire) else sol[i] for i in range(3)]
        if step < 2:
            image = [
                (dire[i] if i < len(dire) else 0.0) - (dire[i - 1] if i else 0.0) for i in range(len(dire) + 1)
            ]
            res = [(res[i] if i < len(res) else 0.0) - alpha * image[i] for i in range(len(image))]
            new = gram(res, res, 0)
            beta = new / rz
            dire = [res[i] + (beta * dire[i] if i < len(dire) else 0.0) for i in range(len(res))]
            rz = new
    surf[...] = sol[0] * press[0, own, :] + sol[1] * press[1, own, :] + sol[2] * press[2, own, :]

    to_east.wait_send()
    to_west.wait_send()
    to_east3.wait_send()
    to_west3.wait_send()

    @pl.when(not_top)
    def _():
        for send in north_sends:
            send.wait_send()
        to_north3.wait_send()

    @pl.when(not_low)
    def _():
        for send in south_sends:
            send.wait_send()
        to_south3.wait_send()

    @pl.when(is_top)
    def _():
        settle(fold2.at[0:NLON - 1, 0:FOLD2, :], group_send.at[0])
        settle(fold3.at[0:NLON - 1], group_send.at[1])

    settle(sums1.at[0:NX * NLAT - 1, :], group_send.at[2])
    settle(sums2.at[0:NZ - 1, :], group_send.at[3])


def store(*refs):
    ins, outs, sem = refs[:5], refs[5:10], refs[10]
    copies = [pltpu.make_async_copy(i, o, sem.at[n]) for n, (i, o) in enumerate(zip(ins, outs))]
    for c in copies:
        c.start()
    for c in copies:
        c.wait()


def body(t, s, u, v, spans, water, opp, weights, anomaly):
    hbm = pl.BlockSpec(memory_space=pltpu.HBM)
    smem = pl.BlockSpec(memory_space=pltpu.SMEM)
    vmem = pl.BlockSpec(memory_space=pltpu.VMEM)
    f32 = jnp.float32
    shapes = [jax.ShapeDtypeStruct((LEVELS, ROWS, LANES), f32)] * 4 + [jax.ShapeDtypeStruct((ROWS, LANES), f32)]
    full = ROWS + 2 * EDGE
    results = pl.pallas_call(
        kernel,
        out_shape=shapes,
        in_specs=[hbm] * 7 + [smem] * 2,
        out_specs=[vmem] * 5,
        scratch_shapes=[
            pltpu.VMEM((2, LEVELS, full, LANES), f32),
            pltpu.VMEM((2, LEVELS, ROWS, LANES), f32),
            pltpu.VMEM((ROWS, LANES), jnp.int32),
            pltpu.VMEM((2, ROWS, LANES), f32),
            pltpu.VMEM((5, 2, full, LANES), f32),
            pltpu.VMEM((ROWS, LANES), f32),
            pltpu.VMEM((2, full, LANES), f32),
            pltpu.VMEM((ROWS, LANES), f32),
            pltpu.VMEM((2, ROWS, LANES), f32),
            pltpu.VMEM((24, LANES), f32),
            pltpu.VMEM((NLON, 24, LANES), f32),
            pltpu.VMEM((FOLD3, LANES), f32),
            pltpu.VMEM((NLON, FOLD3, LANES), f32),
            pltpu.VMEM((3, full, LANES), f32),
            pltpu.VMEM((2 * EDGE, LANES), f32),
            pltpu.VMEM((NX * NLAT, LANES), f32),
            pltpu.VMEM((NZ, LANES), f32),
            pltpu.SemaphoreType.DMA((7,)),
            pltpu.SemaphoreType.DMA((12,)),
            pltpu.SemaphoreType.DMA((12,)),
            pltpu.SemaphoreType.DMA((4,)),
            pltpu.SemaphoreType.DMA((4,)),
        ],
        compiler_params=pltpu.CompilerParams(
            collective_id=0, has_side_effects=True, vmem_limit_bytes=40 * 1024 * 1024
        ),
    )(t, s, u, v, water, weights, anomaly, spans, opp)
    anyspec = pl.BlockSpec(memory_space=pl.ANY)
    return pl.pallas_call(
        store,
        out_shape=shapes,
        in_specs=[anyspec] * 5,
        out_specs=[anyspec] * 5,
        scratch_shapes=[pltpu.SemaphoreType.DMA((5,))],
    )(*results)


def solution(mesh):
    deep = P(None, "lat", "lon")
    flat = P("lat", "lon")
    return jax.shard_map(
        body,
        mesh=mesh,
        in_specs=(deep, deep, deep, deep, P(), flat, P("lon"), flat, flat),
        out_specs=(deep, deep, deep, deep, flat),
        check_vma=False,
    )
```

time: 707 us -> 85.9 us (0.12)
  the two profiles are of different devices: /device:TPU:1 before, /device:TPU:25 now
where the time goes in v1:
time: 85.9 us; the launch traced here: 85.4 us
  Pallas kernels  73.8 us (86%)
  local copies, waits for them, and re-layouts  11 us (13%)
    pallas_call x1, Pallas kernels, body(): pl.pallas_call(store, out_shape=shapes, in_specs=[anyspec] * 5, out_specs...  41.8 us
    pallas_call x1, Pallas kernels, body(): pl.pallas_call(kernel, out_shape=shapes, in_specs=[hbm] * 7 + [smem] * 2,...  31.9 us
    unnamed x28, local copies, waits for them, and re-layouts  11 us

profile of v1, /device:TPU:25, one launch (start us, length us, event | category | flops | bytes accessed | tf_op | source)
XLA Modules:
  0.0 85.4 jit_solution(15894540455419553054)
XLA Ops:
  0.6 0.0 copy-start
  0.6 1.0 %copy-done = f32[10,64,128]{2,1,0:T(8,128)S(1)} copy-done((f32[10,64,128]{2,1,0:T(8,128)S(1)}, f32[10,64,128]{2,1,0:T(8,128)}, u32[]{:S(2)}) %copy-start) | copy-done | bytes 327704
  1.6 0.0 copy-start.1
  1.6 1.0 %copy-done.1 = f32[10,64,128]{2,1,0:T(8,128)S(1)} copy-done((f32[10,64,128]{2,1,0:T(8,128)S(1)}, f32[10,64,128]{2,1,0:T(8,128)}, u32[]{:S(2)}) %copy-start.1) | copy-done | bytes 327704
  2.6 0.0 copy-start.2
  2.6 1.0 %copy-done.2 = f32[10,64,128]{2,1,0:T(8,128)S(1)} copy-done((f32[10,64,128]{2,1,0:T(8,128)S(1)}, f32[10,64,128]{2,1,0:T(8,128)}, u32[]{:S(2)}) %copy-start.2) | copy-done | bytes 327704
  3.6 0.0 copy-start.3
  3.6 1.0 %copy-done.3 = f32[10,64,128]{2,1,0:T(8,128)S(1)} copy-done((f32[10,64,128]{2,1,0:T(8,128)S(1)}, f32[10,64,128]{2,1,0:T(8,128)}, u32[]{:S(2)}) %copy-start.3) | copy-done | bytes 327704
  4.5 0.0 copy-start.8
  4.5 0.8 copy-done.8
  5.3 0.0 copy-start.9
  5.3 0.8 copy-done.9
  6.0 0.0 copy-start.10
  6.0 0.8 copy-done.10
  6.8 0.0 copy-start.12
  6.8 0.7 copy-done.12
  7.5 0.0 copy-start.13
  7.5 0.7 copy-done.13
  8.1 31.9 %shard_map.128 = (f32[10,64,128]{2,1,0:T(8,128)S(1)}, f32[10,64,128]{2,1,0:T(8,128)S(1)}, f32[10,64,128]{2,1,0:T(8,128)S(1)}, f32[10,64,128]{2,1,0:T(8,128)S(1)}, f32[64,128]{1,0:T(8,128)S(1)}) custom-call(f32[10,64,128]{2,1,0:T(8,128)S(1)} %copy-done, f32[10,64,128]{2,1,0:T(8,128)S(1)} %copy-done.1, f32[10,64,128]{2,1,0:T(8,128)S(1)} %copy-done.2, ...), custom_call_target="tpu_custom_call" | custom-call | tf_op jit(solution)/shard_map/pallas_call | solution.py:488
  40.1 0.0 copy-start.4
  40.1 0.7 copy-done.4
  40.8 0.0 copy-start.5
  40.8 0.7 copy-done.5
  41.5 0.0 copy-start.6
  41.5 0.7 copy-done.6
  42.2 0.0 copy-start.7
  42.2 0.7 copy-done.7
  43.0 0.0 copy-start.11
  43.0 0.6 copy-done.11
  43.6 41.8 %shard_map.129 = (f32[10,64,128]{2,1,0:T(8,128)}, f32[10,64,128]{2,1,0:T(8,128)}, f32[10,64,128]{2,1,0:T(8,128)}, f32[10,64,128]{2,1,0:T(8,128)}, f32[64,128]{1,0:T(8,128)}) custom-call(f32[10,64,128]{2,1,0:T(8,128)} %copy-done.4, f32[10,64,128]{2,1,0:T(8,128)} %copy-done.5, f32[10,64,128]{2,1,0:T(8,128)} %copy-done.6, f32[10,64,128]{2,1,0:T(8,128)} %copy-done.7, ...), custom_call_target="tpu_custom_call" | custom-call | tf_op jit(solution)/shard_map/pallas_call | solution.py:522
Async XLA Ops:
  0.6 1.0 %copy-start = (f32[10,64,128]{2,1,0:T(8,128)S(1)}, f32[10,64,128]{2,1,0:T(8,128)}, u32[]{:S(2)}) copy-start(f32[10,64,128]{2,1,0:T(8,128)} %t_hbm.1) | copy-start | bytes 983044
  1.6 1.0 %copy-start.1 = (f32[10,64,128]{2,1,0:T(8,128)S(1)}, f32[10,64,128]{2,1,0:T(8,128)}, u32[]{:S(2)}) copy-start(f32[10,64,128]{2,1,0:T(8,128)} %s_hbm.1) | copy-start | bytes 983044
  2.6 1.0 %copy-start.2 = (f32[10,64,128]{2,1,0:T(8,128)S(1)}, f32[10,64,128]{2,1,0:T(8,128)}, u32[]{:S(2)}) copy-start(f32[10,64,128]{2,1,0:T(8,128)} %u_hbm.1) | copy-start | bytes 983044
  3.6 1.0 %copy-start.3 = (f32[10,64,128]{2,1,0:T(8,128)S(1)}, f32[10,64,128]{2,1,0:T(8,128)}, u32[]{:S(2)}) copy-start(f32[10,64,128]{2,1,0:T(8,128)} %v_hbm.1) | copy-start | bytes 983044
  4.5 0.8 copy-start.8
  5.3 0.8 copy-start.9
  6.0 0.8 copy-start.10
  6.8 0.7 copy-start.12
  7.5 0.7 copy-start.13
  40.1 0.7 copy-start.4
  40.8 0.7 copy-start.5
  41.5 0.7 copy-start.6
  42.2 0.7 copy-start.7
  43.0 0.6 copy-start.11

commit v2 on v1

--- a/solution.py
+++ b/solution.py
@@ -479,6 +479,9 @@
 
 
 def body(t, s, u, v, spans, water, opp, weights, anomaly):
+    t, s, u, v, water, weights, anomaly, spans, opp = (
+        pltpu.with_memory_space_constraint(r, pltpu.HBM) for r in (t, s, u, v, water, weights, anomaly, spans, opp)
+    )
     hbm = pl.BlockSpec(memory_space=pltpu.HBM)
     smem = pl.BlockSpec(memory_space=pltpu.SMEM)
     vmem = pl.BlockSpec(memory_space=pltpu.VMEM)
@@ -525,6 +528,7 @@
         in_specs=[anyspec] * 5,
         out_specs=[anyspec] * 5,
         scratch_shapes=[pltpu.SemaphoreType.DMA((5,))],
+        compiler_params=pltpu.CompilerParams(vmem_limit_bytes=8 * 1024 * 1024),
     )(*results)
 
 

time: 85.9 us -> 33.7 us (0.39)
  Pallas kernels: 73.8 us -> 32.9 us
  local copies, waits for them, and re-layouts: 11 us -> 0 us
    pallas_call x1, Pallas kernels: 41.8 us -> 1.1 us  [body(): pl.pallas_call(store, out_shape=shapes, in_specs=[anyspec] * 5, out_specs...]
    unnamed x28 -> x0, local copies, waits for them, and re-layouts: 11 us -> none
where the time goes in v2:
time: 33.7 us; the launch traced here: 33.6 us
  Pallas kernels  32.9 us (98%)
  between operations  0.64 us (2%)
    pallas_call x1, Pallas kernels, body(): pl.pallas_call(kernel, out_shape=shapes, in_specs=[hbm] * 7 + [smem] * 2,...  31.8 us
    pallas_call x1, Pallas kernels, body(): pl.pallas_call(store, out_shape=shapes, in_specs=[anyspec] * 5, out_specs...  1.1 us

profile of v2, /device:TPU:25, one launch (start us, length us, event | category | flops | bytes accessed | tf_op | source)
XLA Modules:
  0.0 33.6 jit_solution(17699905100394262627)
XLA Ops:
  0.6 31.8 %shard_map.128 = (f32[10,64,128]{2,1,0:T(8,128)S(1)}, f32[10,64,128]{2,1,0:T(8,128)S(1)}, f32[10,64,128]{2,1,0:T(8,128)S(1)}, f32[10,64,128]{2,1,0:T(8,128)S(1)}, f32[64,128]{1,0:T(8,128)S(1)}) custom-call(f32[10,64,128]{2,1,0:T(8,128)} %t_hbm.1, f32[10,64,128]{2,1,0:T(8,128)} %s_hbm.1, f32[10,64,128]{2,1,0:T(8,128)} %u_hbm.1, f32[10,64,128]{2,1,0:T(8,128)} %v_hbm.1, ...), custom_call_target="tpu_custom_call" | custom-call | tf_op jit(solution)/shard_map/pallas_call | solution.py:491
  32.5 1.1 %shard_map.129 = (f32[10,64,128]{2,1,0:T(8,128)}, f32[10,64,128]{2,1,0:T(8,128)}, f32[10,64,128]{2,1,0:T(8,128)}, f32[10,64,128]{2,1,0:T(8,128)}, f32[64,128]{1,0:T(8,128)}) custom-call(f32[10,64,128]{2,1,0:T(8,128)S(1)} %get-tuple-element.10.refs_0_, f32[10,64,128]{2,1,0:T(8,128)S(1)} %get-tuple-element.11.refs_1_, ...), custom_call_target="tpu_custom_call" | custom-call | tf_op jit(solution)/shard_map/pallas_call | solution.py:525

commit v3 on v2

--- a/solution.py
+++ b/solution.py
@@ -18,7 +18,7 @@
 NZ = 8
 SPAN2 = 10
 SPAN3 = 4
-FOLD2 = 20
+FOLD2 = 13
 FOLD3 = 4 * LEVELS
 
 
@@ -33,12 +33,13 @@
 def kernel(
     t_hbm, s_hbm, u_hbm, v_hbm, w_hbm, e_hbm, a_hbm, spans, opp,
     nt, ns, nu, nv, surf,
-    ts, uv, wbuf, ebuf, x, pack, wide, pack3, wide3, own2, fold2, own3, fold3, press, vec, sums1, sums2,
+    ts, uv, wbuf, ebuf, x, pack, wide, pack3, wide3, own2, fold2, own3, foldz, own3x, foldx, press, vec, sums1, sums2,
     in_sem, side_send, side_recv, group_send, group_recv,
 ):
     lon = lax.axis_index("lon")
     lat = lax.axis_index("lat")
     lon_x = lax.rem(lon, NX)
+    lon_z = lax.div(lon, NX)
     east = lax.rem(lon + 1, NLON)
     west = lax.rem(lon + NLON - 1, NLON)
     is_top = lat == NLAT - 1
@@ -127,17 +128,24 @@
 
     @pl.when(is_top)
     def _():
-        row = 0
-        for f, count in ((0, 5), (1, 3), (2, 4), (3, 4), (4, 4)):
-            for r in range(count):
-                last = EDGE + ROWS - 1 - r
-                line = x[f, 0, last:last + 1, :]
-                own2[row:row + 1, :] = -line if f in (1, 2) else line
-                row += 1
+        last = EDGE + ROWS - 1
+        up = x[0, 0, last - 2:last + 1, :]
+        down = x[0, 0, last - 4:last - 1, :]
+        inner = slice(last - 3, last)
+        flow = jnp.where(x[3, 0, inner, :] > 0.0, x[2, 0, inner, :] - 0.05 * (up - down), 0.0)
+        for r in range(3):
+            row = last - r
+            own2[r:r + 1, :] = x[0, 0, row:row + 1, :]
+            own2[3 + r:4 + r, :] = -x[1, 0, row:row + 1, :]
+            half = 0.5 * x[3, 0, row:row + 1, :]
+            own2[7 + r:8 + r, :] = x[3, 0, row:row + 1, :]
+            inside = flow[2 - r:3 - r] if r < 2 else flow[0:1] - flow[2:3]
+            own2[10 + r:11 + r, :] = x[4, 0, row:row + 1, :] + half * inside
+        own2[6:7, :] = -x[2, 0, last:last + 1, :]
         fold2[lon, 0:FOLD2, :] = own2[0:FOLD2, :]
         for q in range(2 * LEVELS):
             own3[2 * q:2 * q + 2, :] = ts[q // LEVELS, q % LEVELS, EDGE + ROWS - 2:EDGE + ROWS, :]
-        fold3[lon] = own3[...]
+        foldz[lon_z] = own3[...]
         for f in range(5):
             x[f, 0, EDGE + ROWS:, :] = jnp.zeros((EDGE, LANES), jnp.float32)
 
@@ -226,10 +234,6 @@
     def _():
         to_south3.start()
 
-    @pl.when(is_top)
-    def _():
-        spread(own3, fold3.at[lon], 1, ring)
-
     to_east.wait_recv()
     to_west.wait_recv()
 
@@ -272,7 +276,7 @@
         kept = lanes_e <= offset
         near_half = index < LANES // 2
         mine, aside = [], []
-        for tile in range(3):
+        for tile in range(2):
             part = slice(EDGE * tile, EDGE * (tile + 1))
             b_p, b_0, b_m, b_mm = (fold2[s, part, :] for s in (slot_p, slot, slot_m, slot_mm))
             mine.append(turn(jnp.where(kept, b_0, b_m)))
@@ -280,11 +284,13 @@
             left = jnp.where(kept, b_p, b_0)
             aside.append(turn(jnp.where(near_half, right, left)))
         for half, tiles in ((0, mine), (1, aside)):
-            x[0, half, EDGE + ROWS:EDGE + ROWS + 5, :] = tiles[0][0:5]
-            x[1, half, EDGE + ROWS:EDGE + ROWS + 3, :] = tiles[0][5:8]
-            x[2, half, EDGE + ROWS:EDGE + ROWS + 4, :] = tiles[1][0:4]
-            x[3, half, EDGE + ROWS:EDGE + ROWS + 4, :] = tiles[1][4:8]
-            x[4, half, EDGE + ROWS:EDGE + ROWS + 4, :] = tiles[2][0:4]
+            north = EDGE + ROWS
+            x[0, half, north:north + 3, :] = tiles[0][0:3]
+            x[1, half, north:north + 3, :] = tiles[0][3:6]
+            x[2, half, north:north + 1, :] = tiles[0][6:7]
+            x[3, half, north:north + 1, :] = tiles[0][7:8]
+            x[3, half, north + 1:north + 3, :] = tiles[1][0:2]
+            x[4, half, north:north + 3, :] = tiles[1][2:5]
 
     full = EDGE + ROWS + EDGE
     first_lane = lanes_w == 0
@@ -314,9 +320,11 @@
     q_e = plus_east(*q2)
     q_w = plus_west(*q2)
     flow_e, flow_n = [], []
+    rows_w = lax.broadcasted_iota(jnp.int32, (full, LANES), 0)
+    rows_end = jnp.where(is_top, EDGE + ROWS, full)
     for h in range(2):
         flow_e.append(jnp.where(wet2[h], x[1, h] - 0.05 * (q_e[h] - q_w[h]), 0.0))
-        flow_n.append(jnp.where(wet2[h], x[2, h] - 0.05 * (north_of(q2[h]) - south_of(q2[h])), 0.0))
+        flow_n.append(jnp.where(wet2[h] & (rows_w <= rows_end), x[2, h] - 0.05 * (north_of(q2[h]) - south_of(q2[h])), 0.0))
     f_e = plus_east(*flow_e)
     f_w = plus_west(*flow_e)
     basis = []
@@ -347,6 +355,10 @@
     sums1[pl.ds(mine1, 1), :] = message
     spread(vec.at[0:1, :], sums1.at[pl.ds(mine1, 1), :], 2, near)
 
+    @pl.when(is_top)
+    def _():
+        spread(own3, foldz.at[lon_z], 1, far)
+
     to_east3.wait_recv()
     to_west3.wait_recv()
 
@@ -358,62 +370,76 @@
     def _():
         to_south3.wait_recv()
 
-    @pl.when(is_top)
-    def _():
-        settle(fold3.at[0:NLON - 1], group_recv.at[1])
-        kept = lanes_e <= offset
-        for tile in range(FOLD3 // EDGE):
-            part = slice(EDGE * tile, EDGE * (tile + 1))
-            turned = turn(jnp.where(kept, fold3[slot, part, :], fold3[slot_m, part, :]))
-            for i in range(EDGE):
-                q, r = (EDGE * tile + i) // 2, (EDGE * tile + i) % 2
-                ts[q // LEVELS, q % LEVELS, EDGE + ROWS + 1 - r:EDGE + ROWS + 2 - r, :] = turned[i:i + 1]
-
-    merged3 = jnp.where((lanes & 2) == 0, wide3[0], wide3[1])
-    below = jnp.zeros((full, LANES), jnp.float32)
-    below_side = zero
-    tracer_out = (nt, ns)
-    for k in range(LEVELS):
-        span = spans[k]
-        u = uv[0, k]
-        w = uv[1, k]
-        sides = []
-        for f in range(2):
-            side = pltpu.roll(merged3, LANES - (SPAN3 * (f * LEVELS + k) + 2), 1)
-            sides.append(side)
-            c = ts[f, k, EDGE:EDGE + ROWS, :]
-            e1 = pltpu.roll(jnp.where(lanes == 0, side, c), LANES - 1, 1)
-            e2 = pltpu.roll(jnp.where(lanes < 2, side, c), LANES - 2, 1)
-            w1 = pltpu.roll(jnp.where(lanes == LANES - 1, side, c), 1, 1)
-            w2 = pltpu.roll(jnp.where(lanes >= LANES - 2, side, c), 2, 1)
-            n1 = ts[f, k, EDGE + 1:EDGE + ROWS + 1, :]
-            n2 = ts[f, k, EDGE + 2:EDGE + ROWS + 2, :]
-            s1 = ts[f, k, EDGE - 1:EDGE + ROWS - 1, :]
-            s2 = ts[f, k, EDGE - 2:EDGE + ROWS - 2, :]
-            grad_e = (8.0 * (e1 - w1) - (e2 - w2)) * (1.0 / 12.0)
-            grad_n = (8.0 * (n1 - s1) - (n2 - s2)) * (1.0 / 12.0)
-            laplace = e1 + w1 + n1 + s1 - 4.0 * c
-            tracer_out[f][k] = c + wetness * (-0.1 * (u * grad_e + w * grad_n) + 0.1 * laplace)
-        layer = density(ts[0, k], ts[1, k]) * span
-        level = below + 0.5 * layer
-        below = below + layer
-        layer_side = density(sides[0], sides[1]) * span
-        level_side = below_side + 0.5 * layer_side
-        below_side = below_side + layer_side
-        centre = level[EDGE:EDGE + ROWS]
-        p_e = pltpu.roll(jnp.where(lanes == 0, level_side, centre), LANES - 1, 1)
-        p_w = pltpu.roll(jnp.where(lanes == LANES - 1, level_side, centre), 1, 1)
-        p_n = north_of(level)[EDGE:EDGE + ROWS]
-        p_s = south_of(level)[EDGE:EDGE + ROWS]
-        nu[k] = wetness * (u - 0.05 * (p_e - p_w))
-        nv[k] = wetness * (w - 0.05 * (p_n - p_s))
+    def update(low, rows, parts):
+        lane = lane_iota(rows)
+        part = slice(low, low + rows)
+        wet = wbuf[part, :].astype(jnp.float32)
+        joined = jnp.where((lane & 2) == 0, wide3[0, part, :], wide3[1, part, :])
+        below = jnp.zeros((rows + 2 * EDGE, LANES), jnp.float32)
+        below_side = jnp.zeros((rows, LANES), jnp.float32)
+        mid = slice(EDGE, EDGE + rows)
+        for k in range(LEVELS):
+            span = spans[k]
+            u = uv[0, k, part, :]
+            w = uv[1, k, part, :]
+            sides = []
+            for f in range(2):
+                side = pltpu.roll(joined, LANES - (SPAN3 * (f * LEVELS + k) + 2), 1)
+                sides.append(side)
+                at = EDGE + low
+                c = ts[f, k, at:at + rows, :]
+                e1 = pltpu.roll(jnp.where(lane == 0, side, c), LANES - 1, 1)
+                e2 = pltpu.roll(jnp.where(lane < 2, side, c), LANES - 2, 1)
+                w1 = pltpu.roll(jnp.where(lane == LANES - 1, side, c), 1, 1)
+                w2 = pltpu.roll(jnp.where(lane >= LANES - 2, side, c), 2, 1)
+                n1 = ts[f, k, at + 1:at + rows + 1, :]
+                n2 = ts[f, k, at + 2:at + rows + 2, :]
+                s1 = ts[f, k, at - 1:at + rows - 1, :]
+                s2 = ts[f, k, at - 2:at + rows - 2, :]
+                grad_e = (8.0 * (e1 - w1) - (e2 - w2)) * (1.0 / 12.0)
+                grad_n = (8.0 * (n1 - s1) - (n2 - s2)) * (1.0 / 12.0)
+                laplace = e1 + w1 + n1 + s1 - 4.0 * c
+                out = (nt, ns)[f]
+                out[k, part, :] = c + wet * (-0.1 * (u * grad_e + w * grad_n) + 0.1 * laplace)
+            reach = slice(low, low + rows + 2 * EDGE)
+            layer = density(ts[0, k, reach, :], ts[1, k, reach, :]) * span
+            level = below + 0.5 * layer
+            below = below + layer
+            p_n = pltpu.roll(level, rows + 2 * EDGE - 1, 0)[mid]
+            p_s = pltpu.roll(level, 1, 0)[mid]
+            nv[k, part, :] = wet * (w - 0.05 * (p_n - p_s))
+            if parts > 1:
+                layer_side = density(sides[0], sides[1]) * span
+                level_side = below_side + 0.5 * layer_side
+                below_side = below_side + layer_side
+                centre = level[mid]
+                p_e = pltpu.roll(jnp.where(lane == 0, level_side, centre), LANES - 1, 1)
+                p_w = pltpu.roll(jnp.where(lane == LANES - 1, level_side, centre), 1, 1)
+                nu[k, part, :] = wet * (u - 0.05 * (p_e - p_w))
+
+    update(0, ROWS, 2)
 
     settle(sums1.at[0:NX * NLAT - 1, :], group_recv.at[2])
     total = jnp.sum(sums1[...], axis=0, keepdims=True)
-    mine2 = lax.div(lon, NX)
+    mine2 = lon_z
     vec[EDGE:EDGE + 1, :] = total
     sums2[pl.ds(mine2, 1), :] = total
     spread(vec.at[EDGE:EDGE + 1, :], sums2.at[pl.ds(mine2, 1), :], 3, far)
+
+    beside = [(lon - lon_x + lax.rem(lon_x + k, NX), lat) for k in range(1, NX)]
+    kept = lane_iota(FOLD3) <= offset
+
+    @pl.when(is_top)
+    def _():
+        settle(foldz.at[0:NZ - 1], group_recv.at[1])
+        base_slot = slot + lon_x + NLON
+        row_0 = lax.div(lax.rem(base_slot - (slot & (NX - 1)), NLON), NX)
+        row_1 = lax.div(lax.rem(base_slot - 1 - ((slot + NX - 1) & (NX - 1)), NLON), NX)
+        joint = jnp.where(kept, foldz[row_0], foldz[row_1])
+        own3x[...] = joint
+        foldx[lon_x] = joint
+        spread(own3x, foldx.at[lon_x], 4, beside)
+
     settle(sums2.at[0:NZ - 1, :], group_recv.at[3])
     total = jnp.sum(sums2[...], axis=0, keepdims=True)
     mu = [total[:, j:j + 1] for j in range(6)]
@@ -443,6 +469,19 @@
             rz = new
     surf[...] = sol[0] * press[0, own, :] + sol[1] * press[1, own, :] + sol[2] * press[2, own, :]
 
+    @pl.when(is_top)
+    def _():
+        settle(foldx.at[0:NX - 1], group_recv.at[4])
+        side_0 = slot & (NX - 1)
+        side_1 = (slot + NX - 1) & (NX - 1)
+        for tile in range(FOLD3 // EDGE):
+            part = slice(EDGE * tile, EDGE * (tile + 1))
+            turned = turn(jnp.where(kept[part], foldx[side_0, part, :], foldx[side_1, part, :]))
+            for i in range(EDGE):
+                q, r = (EDGE * tile + i) // 2, (EDGE * tile + i) % 2
+                ts[q // LEVELS, q % LEVELS, EDGE + ROWS + 1 - r:EDGE + ROWS + 2 - r, :] = turned[i:i + 1]
+        update(ROWS - EDGE, EDGE, 1)
+
     to_east.wait_send()
     to_west.wait_send()
     to_east3.wait_send()
@@ -463,7 +502,8 @@
     @pl.when(is_top)
     def _():
         settle(fold2.at[0:NLON - 1, 0:FOLD2, :], group_send.at[0])
-        settle(fold3.at[0:NLON - 1], group_send.at[1])
+        settle(foldz.at[0:NZ - 1], group_send.at[1])
+        settle(foldx.at[0:NX - 1], group_send.at[4])
 
     settle(sums1.at[0:NX * NLAT - 1, :], group_send.at[2])
     settle(sums2.at[0:NZ - 1, :], group_send.at[3])
@@ -503,10 +543,12 @@
             pltpu.VMEM((2, full, LANES), f32),
             pltpu.VMEM((ROWS, LANES), f32),
             pltpu.VMEM((2, ROWS, LANES), f32),
-            pltpu.VMEM((24, LANES), f32),
-            pltpu.VMEM((NLON, 24, LANES), f32),
+            pltpu.VMEM((16, LANES), f32),
+            pltpu.VMEM((NLON, 16, LANES), f32),
             pltpu.VMEM((FOLD3, LANES), f32),
-            pltpu.VMEM((NLON, FOLD3, LANES), f32),
+            pltpu.VMEM((NZ, FOLD3, LANES), f32),
+            pltpu.VMEM((FOLD3, LANES), f32),
+            pltpu.VMEM((NX, FOLD3, LANES), f32),
             pltpu.VMEM((3, full, LANES), f32),
             pltpu.VMEM((2 * EDGE, LANES), f32),
             pltpu.VMEM((NX * NLAT, LANES), f32),
@@ -514,8 +556,8 @@
             pltpu.SemaphoreType.DMA((7,)),
             pltpu.SemaphoreType.DMA((12,)),
             pltpu.SemaphoreType.DMA((12,)),
-            pltpu.SemaphoreType.DMA((4,)),
-            pltpu.SemaphoreType.DMA((4,)),
+            pltpu.SemaphoreType.DMA((5,)),
+            pltpu.SemaphoreType.DMA((5,)),
         ],
         compiler_params=pltpu.CompilerParams(
             collective_id=0, has_side_effects=True, vmem_limit_bytes=40 * 1024 * 1024

time: 33.7 us -> 30.2 us (0.90)
  the two profiles are of different devices: /device:TPU:25 before, /device:TPU:1 now
where the time goes in v3:
time: 30.2 us; the launch traced here: 30.1 us
  Pallas kernels  29.5 us (98%)
  between operations  0.64 us (2%)
    pallas_call x1, Pallas kernels, body(): pl.pallas_call(kernel, out_shape=shapes, in_specs=[hbm] * 7 + [smem] * 2,...  28.4 us
    pallas_call x1, Pallas kernels, body(): pl.pallas_call(store, out_shape=shapes, in_specs=[anyspec] * 5, out_specs...  1.1 us

profile of v3, /device:TPU:1, one launch (start us, length us, event | category | flops | bytes accessed | tf_op | source)
XLA Modules:
  0.0 30.1 jit_solution(4179992745252972013)
XLA Ops:
  0.6 28.4 %shard_map.128 = (f32[10,64,128]{2,1,0:T(8,128)S(1)}, f32[10,64,128]{2,1,0:T(8,128)S(1)}, f32[10,64,128]{2,1,0:T(8,128)S(1)}, f32[10,64,128]{2,1,0:T(8,128)S(1)}, f32[64,128]{1,0:T(8,128)S(1)}) custom-call(f32[10,64,128]{2,1,0:T(8,128)} %t_hbm.1, f32[10,64,128]{2,1,0:T(8,128)} %s_hbm.1, f32[10,64,128]{2,1,0:T(8,128)} %u_hbm.1, f32[10,64,128]{2,1,0:T(8,128)} %v_hbm.1, ...), custom_call_target="tpu_custom_call" | custom-call | tf_op jit(solution)/shard_map/pallas_call | solution.py:531
  29.0 1.1 %shard_map.129 = (f32[10,64,128]{2,1,0:T(8,128)}, f32[10,64,128]{2,1,0:T(8,128)}, f32[10,64,128]{2,1,0:T(8,128)}, f32[10,64,128]{2,1,0:T(8,128)}, f32[64,128]{1,0:T(8,128)}) custom-call(f32[10,64,128]{2,1,0:T(8,128)S(1)} %get-tuple-element.10.refs_0_, f32[10,64,128]{2,1,0:T(8,128)S(1)} %get-tuple-element.11.refs_1_, ...), custom_call_target="tpu_custom_call" | custom-call | tf_op jit(solution)/shard_map/pallas_call | solution.py:567

commit v4 on v3

--- a/solution.py
+++ b/solution.py
@@ -1,4 +1,4 @@
-import functools
+import itertools
 
 import jax
 import jax.numpy as jnp
@@ -47,6 +47,58 @@
     not_top = lat < NLAT - 1
     not_low = lat > 0
 
+    barrier = pltpu.get_barrier_semaphore()
+
+    def greet(dev):
+        pl.semaphore_signal(barrier, inc=1, device_id=dev, device_id_type=MESH)
+
+    def hops(step, size):
+        return min(step, size - step)
+
+    lat_y = lax.div(lat, 2)
+    lat_c = lat & 1
+    zs = [((lon_z + d) & (NZ - 1)) * NX for d in range(NZ)]
+    xs = [(lon_x + d) & (NX - 1) for d in range(NX)]
+    lats = {(dy, dc): ((lat_y + dy) & (NLAT // 2 - 1)) * 2 + (lat_c ^ dc) for dy in range(NLAT // 2) for dc in range(2)}
+
+    def at(dz, dx, dy, dc):
+        return (zs[dz] + xs[dx], lats[dy, dc])
+
+    near = [
+        at(0, dx, dy, dc)
+        for dx, dy, dc in sorted(
+            itertools.product(range(NX), range(NLAT // 2), range(2)),
+            key=lambda o: -hops(o[0], NX) - hops(o[1], NLAT // 2) - 0.5 * o[2],
+        )
+        if dx or dy or dc
+    ]
+    far = [at(dz, 0, 0, 0) for dz in sorted(range(1, NZ), key=lambda o: -hops(o, NZ))]
+    ring = [
+        at(dz, dx, 0, 0)
+        for dz, dx in sorted(
+            itertools.product(range(NZ), range(NX)), key=lambda o: -hops(o[0], NZ) - hops(o[1], NX)
+        )
+        if dz or dx
+    ]
+
+    @pl.when(is_top)
+    def _():
+        for dev in ring:
+            greet(dev)
+
+    for dev in far + near + [(east, lat), (west, lat)]:
+        greet(dev)
+
+    @pl.when(not_top)
+    def _():
+        greet((east, lat + 1))
+        greet((west, lat + 1))
+
+    @pl.when(not_low)
+    def _():
+        greet((east, lat - 1))
+        greet((west, lat - 1))
+
     loads = [
         pltpu.make_async_copy(w_hbm, wbuf, in_sem.at[0]),
         pltpu.make_async_copy(e_hbm, ebuf.at[0], in_sem.at[1]),
@@ -58,36 +110,6 @@
     ]
     for load in loads:
         load.start()
-
-    barrier = pltpu.get_barrier_semaphore()
-
-    def greet(dev):
-        pl.semaphore_signal(barrier, inc=1, device_id=dev, device_id_type=MESH)
-
-    near = []
-    for dx in range(NX):
-        for dy in range(NLAT):
-            if dx or dy:
-                near.append((lon - lon_x + lax.rem(lon_x + dx, NX), lax.rem(lat + dy, NLAT)))
-    far = [(lax.rem(lon + NX * k, NLON), lat) for k in range(1, NZ)]
-    ring = [(lax.rem(lon + k, NLON), lat) for k in range(1, NLON)]
-    for dev in near + far + [(east, lat), (west, lat)]:
-        greet(dev)
-
-    @pl.when(not_top)
-    def _():
-        greet((east, lat + 1))
-        greet((west, lat + 1))
-
-    @pl.when(not_low)
-    def _():
-        greet((east, lat - 1))
-        greet((west, lat - 1))
-
-    @pl.when(is_top)
-    def _():
-        for dev in ring:
-            greet(dev)
 
     for load in loads[:3]:
         load.wait()

time: 30.2 us -> 28.7 us (0.950)
  Pallas kernels: 29.5 us -> 28 us
    pallas_call x1, Pallas kernels: 28.4 us -> 26.9 us  [body(): pl.pallas_call(kernel, out_shape=shapes, in_specs=[hbm] * 7 + [smem] * 2,...]
where the time goes in v4:
time: 28.7 us; the launch traced here: 28.6 us
  Pallas kernels  28 us (98%)
  between operations  0.64 us (2%)
    pallas_call x1, Pallas kernels, body(): pl.pallas_call(kernel, out_shape=shapes, in_specs=[hbm] * 7 + [smem] * 2,...  26.9 us
    pallas_call x1, Pallas kernels, body(): pl.pallas_call(store, out_shape=shapes, in_specs=[anyspec] * 5, out_specs...  1.1 us

profile of v4, /device:TPU:1, one launch (start us, length us, event | category | flops | bytes accessed | tf_op | source)
XLA Modules:
  0.0 28.6 jit_solution(7035354809605677716)
XLA Ops:
  0.6 26.9 %shard_map.128 = (f32[10,64,128]{2,1,0:T(8,128)S(1)}, f32[10,64,128]{2,1,0:T(8,128)S(1)}, f32[10,64,128]{2,1,0:T(8,128)S(1)}, f32[10,64,128]{2,1,0:T(8,128)S(1)}, f32[64,128]{1,0:T(8,128)S(1)}) custom-call(f32[10,64,128]{2,1,0:T(8,128)} %t_hbm.1, f32[10,64,128]{2,1,0:T(8,128)} %s_hbm.1, f32[10,64,128]{2,1,0:T(8,128)} %u_hbm.1, f32[10,64,128]{2,1,0:T(8,128)} %v_hbm.1, ...), custom_call_target="tpu_custom_call" | custom-call | tf_op jit(solution)/shard_map/pallas_call | solution.py:553
  27.5 1.1 %shard_map.129 = (f32[10,64,128]{2,1,0:T(8,128)}, f32[10,64,128]{2,1,0:T(8,128)}, f32[10,64,128]{2,1,0:T(8,128)}, f32[10,64,128]{2,1,0:T(8,128)}, f32[64,128]{1,0:T(8,128)}) custom-call(f32[10,64,128]{2,1,0:T(8,128)S(1)} %get-tuple-element.10.refs_0_, f32[10,64,128]{2,1,0:T(8,128)S(1)} %get-tuple-element.11.refs_1_, ...), custom_call_target="tpu_custom_call" | custom-call | tf_op jit(solution)/shard_map/pallas_call | solution.py:589

commit v5 on v4

--- a/solution.py
+++ b/solution.py
@@ -31,10 +31,10 @@
 
 
 def kernel(
-    t_hbm, s_hbm, u_hbm, v_hbm, w_hbm, e_hbm, a_hbm, spans, opp,
+    t_hbm, s_hbm, u_hbm, v_hbm, w_hbm, e_hbm, a_hbm, spans_hbm, opp_hbm,
     nt, ns, nu, nv, surf,
-    ts, uv, wbuf, ebuf, x, pack, wide, pack3, wide3, own2, fold2, own3, foldz, own3x, foldx, press, vec, sums1, sums2,
-    in_sem, side_send, side_recv, group_send, group_recv,
+    ts, uv, wbuf, ebuf, x, pack, slim, heard, wide, pack3, wide3, own2, fold2, own3, foldz, own3x, foldx, press, vec, sums1, sums2,
+    spans, opp, in_sem, side_send, side_recv, group_send, group_recv,
 ):
     lon = lax.axis_index("lon")
     lat = lax.axis_index("lat")
@@ -107,6 +107,8 @@
         pltpu.make_async_copy(s_hbm, ts.at[1, :, EDGE:EDGE + ROWS, :], in_sem.at[4]),
         pltpu.make_async_copy(u_hbm, uv.at[0], in_sem.at[5]),
         pltpu.make_async_copy(v_hbm, uv.at[1], in_sem.at[6]),
+        pltpu.make_async_copy(spans_hbm, spans, in_sem.at[7]),
+        pltpu.make_async_copy(opp_hbm, opp, in_sem.at[8]),
     ]
     for load in loads:
         load.start()
@@ -142,11 +144,22 @@
         moved = pltpu.roll(x[f, 0, own, :], SPAN2 * f + 5, 1)
         packed = jnp.where((lanes >= SPAN2 * f) & (lanes < SPAN2 * (f + 1)), moved, packed)
     pack[...] = packed
+    half = ROWS // 2
+    quarter = ROWS // 4
+    lanes_h = lane_iota(half)
+    lanes_q = lane_iota(quarter)
+    eastern = lax.rem(lanes_h, SPAN2) < 5
+    for side, turned in ((0, SPAN2 - 5), (1, LANES - 5)):
+        lower = pltpu.roll(packed[half:], turned, 1)
+        folded = jnp.where(eastern, packed[:half], lower) if side == 0 else jnp.where(eastern, lower, packed[:half])
+        slim[side] = jnp.where(lanes_q < LANES // 2, folded[:quarter], pltpu.roll(folded[quarter:], LANES // 2, 1))
     packed = zero
     for q in range(2 * LEVELS):
         moved = pltpu.roll(ts[q // LEVELS, q % LEVELS, own, :], SPAN3 * q + 2, 1)
         packed = jnp.where((lanes >= SPAN3 * q) & (lanes < SPAN3 * (q + 1)), moved, packed)
-    pack3[...] = packed
+    outer = (lanes_h & 2) == 0
+    pack3[0] = jnp.where(outer, packed[:half], pltpu.roll(packed[half:], 2, 1))
+    pack3[1] = jnp.where(outer, pltpu.roll(packed[half:], LANES - 2, 1), packed[:half])
 
     @pl.when(is_top)
     def _():
@@ -199,16 +212,16 @@
         )
 
     top_rows = slice(EDGE + ROWS, EDGE + ROWS + EDGE)
-    to_east = copy(pack, wide.at[0, own, :], 0, (east, lat))
-    to_west = copy(pack, wide.at[1, own, :], 1, (west, lat))
+    to_east = copy(slim.at[0], heard.at[0], 0, (east, lat))
+    to_west = copy(slim.at[1], heard.at[1], 1, (west, lat))
     to_north = copy(x.at[:, 0, ROWS:EDGE + ROWS, :], x.at[:, 0, 0:EDGE, :], 2, (lon, lat + 1))
-    to_ne = copy(pack.at[ROWS - EDGE:ROWS, :], wide.at[0, 0:EDGE, :], 3, (east, lat + 1))
-    to_nw = copy(pack.at[ROWS - EDGE:ROWS, :], wide.at[1, 0:EDGE, :], 4, (west, lat + 1))
+    to_ne = copy(pack.at[ROWS - EDGE:ROWS, :], wide.at[0, 0], 3, (east, lat + 1))
+    to_nw = copy(pack.at[ROWS - EDGE:ROWS, :], wide.at[1, 0], 4, (west, lat + 1))
     to_south = copy(x.at[:, 0, EDGE:2 * EDGE, :], x.at[:, 0, top_rows, :], 5, (lon, lat - 1))
-    to_se = copy(pack.at[0:EDGE, :], wide.at[0, top_rows, :], 6, (east, lat - 1))
-    to_sw = copy(pack.at[0:EDGE, :], wide.at[1, top_rows, :], 7, (west, lat - 1))
-    to_east3 = copy(pack3, wide3.at[0], 8, (east, lat))
-    to_west3 = copy(pack3, wide3.at[1], 9, (west, lat))
+    to_se = copy(pack.at[0:EDGE, :], wide.at[0, 1], 6, (east, lat - 1))
+    to_sw = copy(pack.at[0:EDGE, :], wide.at[1, 1], 7, (west, lat - 1))
+    to_east3 = copy(pack3.at[0], wide3.at[0], 8, (east, lat))
+    to_west3 = copy(pack3.at[1], wide3.at[1], 9, (west, lat))
     to_north3 = copy(
         ts.at[:, :, EDGE + ROWS - 2:EDGE + ROWS, :], ts.at[:, :, EDGE - 2:EDGE, :], 10, (lon, lat + 1)
     )
@@ -270,8 +283,14 @@
             send.wait_recv()
 
     lanes_w = lane_iota(EDGE + ROWS + EDGE)
-    eastern = lax.rem(lanes_w, SPAN2) < 5
-    merged = jnp.where(eastern, wide[0], wide[1])
+    from_west, from_east = (
+        jnp.concatenate([heard[side], pltpu.roll(heard[side], LANES // 2, 1)], axis=0) for side in range(2)
+    )
+    upper = jnp.where(eastern, from_west, from_east)
+    lower = jnp.where(eastern, pltpu.roll(from_west, LANES - 5, 1), pltpu.roll(from_east, 5, 1))
+    eastern_e = lax.rem(lane_iota(EDGE), SPAN2) < 5
+    corners = [jnp.where(eastern_e, wide[0, c], wide[1, c]) for c in range(2)]
+    merged = jnp.concatenate([corners[0], upper, lower, corners[1]], axis=0)
     for f in range(5):
         x[f, 1] = pltpu.roll(merged, LANES - (SPAN2 * f + 5), 1)
 
@@ -396,7 +415,14 @@
         lane = lane_iota(rows)
         part = slice(low, low + rows)
         wet = wbuf[part, :].astype(jnp.float32)
-        joined = jnp.where((lane & 2) == 0, wide3[0, part, :], wide3[1, part, :])
+        rows_3 = []
+        if low < ROWS // 2:
+            rows_3.append(jnp.where(outer, wide3[0], wide3[1]))
+        cut = max(low - ROWS // 2, 0)
+        low_w = pltpu.roll(wide3[0, cut:, :], LANES - 2, 1)
+        low_e = pltpu.roll(wide3[1, cut:, :], 2, 1)
+        rows_3.append(jnp.where(outer[cut:], low_w, low_e))
+        joined = jnp.concatenate(rows_3, axis=0)
         below = jnp.zeros((rows + 2 * EDGE, LANES), jnp.float32)
         below_side = jnp.zeros((rows, LANES), jnp.float32)
         mid = slice(EDGE, EDGE + rows)
@@ -545,7 +571,6 @@
         pltpu.with_memory_space_constraint(r, pltpu.HBM) for r in (t, s, u, v, water, weights, anomaly, spans, opp)
     )
     hbm = pl.BlockSpec(memory_space=pltpu.HBM)
-    smem = pl.BlockSpec(memory_space=pltpu.SMEM)
     vmem = pl.BlockSpec(memory_space=pltpu.VMEM)
     f32 = jnp.float32
     shapes = [jax.ShapeDtypeStruct((LEVELS, ROWS, LANES), f32)] * 4 + [jax.ShapeDtypeStruct((ROWS, LANES), f32)]
@@ -553,7 +578,7 @@
     results = pl.pallas_call(
         kernel,
         out_shape=shapes,
-        in_specs=[hbm] * 7 + [smem] * 2,
+        in_specs=[hbm] * 9,
         out_specs=[vmem] * 5,
         scratch_shapes=[
             pltpu.VMEM((2, LEVELS, full, LANES), f32),
@@ -562,9 +587,11 @@
             pltpu.VMEM((2, ROWS, LANES), f32),
             pltpu.VMEM((5, 2, full, LANES), f32),
             pltpu.VMEM((ROWS, LANES), f32),
-            pltpu.VMEM((2, full, LANES), f32),
-            pltpu.VMEM((ROWS, LANES), f32),
-            pltpu.VMEM((2, ROWS, LANES), f32),
+            pltpu.VMEM((2, ROWS // 4, LANES), f32),
+            pltpu.VMEM((2, ROWS // 4, LANES), f32),
+            pltpu.VMEM((2, 2, EDGE, LANES), f32),
+            pltpu.VMEM((2, ROWS // 2, LANES), f32),
+            pltpu.VMEM((2, ROWS // 2, LANES), f32),
             pltpu.VMEM((16, LANES), f32),
             pltpu.VMEM((NLON, 16, LANES), f32),
             pltpu.VMEM((FOLD3, LANES), f32),
@@ -575,7 +602,9 @@
             pltpu.VMEM((2 * EDGE, LANES), f32),
             pltpu.VMEM((NX * NLAT, LANES), f32),
             pltpu.VMEM((NZ, LANES), f32),
-            pltpu.SemaphoreType.DMA((7,)),
+            pltpu.SMEM((LEVELS,), f32),
+            pltpu.SMEM((LANES,), jnp.int32),
+            pltpu.SemaphoreType.DMA((9,)),
             pltpu.SemaphoreType.DMA((12,)),
             pltpu.SemaphoreType.DMA((12,)),
             pltpu.SemaphoreType.DMA((5,)),

time: 28.7 us -> 27.7 us (0.965)
  Pallas kernels: 28 us -> 26.9 us
    pallas_call x1, Pallas kernels: 26.9 us -> 25.8 us  [body(): pl.pallas_call(kernel, out_shape=shapes, in_specs=[hbm] * 9, out_specs=[v...]
where the time goes in v5:
time: 27.7 us; the launch traced here: 27.6 us
  Pallas kernels  26.9 us (97%)
  between operations  0.64 us (2%)
    pallas_call x1, Pallas kernels, body(): pl.pallas_call(kernel, out_shape=shapes, in_specs=[hbm] * 9, out_specs=[v...  25.8 us
    pallas_call x1, Pallas kernels, body(): pl.pallas_call(store, out_shape=shapes, in_specs=[anyspec] * 5, out_specs...  1.1 us

profile of v5, /device:TPU:1, one launch (start us, length us, event | category | flops | bytes accessed | tf_op | source)
XLA Modules:
  0.0 27.6 jit_solution(11568872037245900797)
XLA Ops:
  0.6 25.8 %shard_map.128 = (f32[10,64,128]{2,1,0:T(8,128)S(1)}, f32[10,64,128]{2,1,0:T(8,128)S(1)}, f32[10,64,128]{2,1,0:T(8,128)S(1)}, f32[10,64,128]{2,1,0:T(8,128)S(1)}, f32[64,128]{1,0:T(8,128)S(1)}) custom-call(f32[10,64,128]{2,1,0:T(8,128)} %t_hbm.1, f32[10,64,128]{2,1,0:T(8,128)} %s_hbm.1, f32[10,64,128]{2,1,0:T(8,128)} %u_hbm.1, f32[10,64,128]{2,1,0:T(8,128)} %v_hbm.1, ...), custom_call_target="tpu_custom_call" | custom-call | tf_op jit(solution)/shard_map/pallas_call | solution.py:578
  26.5 1.1 %shard_map.129 = (f32[10,64,128]{2,1,0:T(8,128)}, f32[10,64,128]{2,1,0:T(8,128)}, f32[10,64,128]{2,1,0:T(8,128)}, f32[10,64,128]{2,1,0:T(8,128)}, f32[64,128]{1,0:T(8,128)}) custom-call(f32[10,64,128]{2,1,0:T(8,128)S(1)} %get-tuple-element.10.refs_0_, f32[10,64,128]{2,1,0:T(8,128)S(1)} %get-tuple-element.11.refs_1_, ...), custom_call_target="tpu_custom_call" | custom-call | tf_op jit(solution)/shard_map/pallas_call | solution.py:618

commit v6 on v5

--- a/solution.py
+++ b/solution.py
@@ -16,6 +16,7 @@
 NLAT = 8
 NX = 4
 NZ = 8
+EARLY = 2
 SPAN2 = 10
 SPAN3 = 4
 FOLD2 = 13
@@ -33,7 +34,7 @@
 def kernel(
     t_hbm, s_hbm, u_hbm, v_hbm, w_hbm, e_hbm, a_hbm, spans_hbm, opp_hbm,
     nt, ns, nu, nv, surf,
-    ts, uv, wbuf, ebuf, x, pack, slim, heard, wide, pack3, wide3, own2, fold2, own3, foldz, own3x, foldx, press, vec, sums1, sums2,
+    ts, uv, wbuf, ebuf, x, pack, slim, heard, wide, pack3, wide3, own2, fold2, own3, foldz, own3x, foldx, press, rim, vec, sums1, sums2, late1, crown, wide_sent,
     spans, opp, in_sem, side_send, side_recv, group_send, group_recv,
 ):
     lon = lax.axis_index("lon")
@@ -81,10 +82,25 @@
         if dz or dx
     ]
 
+    is_early = lon_z < EARLY
+    crowns = [
+        ((zs[dz] + xs[dx], NLAT - 1), dz or dx) for dz, dx in itertools.product(range(NZ), range(NX))
+    ]
+
     @pl.when(is_top)
     def _():
         for dev in ring:
             greet(dev)
+
+    @pl.when(is_early)
+    def _():
+        for dev, other in crowns:
+            if other:
+                greet(dev)
+
+    @pl.when(is_early & not_top)
+    def _():
+        greet((lon, NLAT - 1))
 
     for dev in far + near + [(east, lat), (west, lat)]:
         greet(dev)
@@ -193,9 +209,15 @@
 
     base = 31 + 7 + 2
 
-    @pl.when(is_top)
-    def _():
-        pl.semaphore_wait(barrier, base + 2 + NLON - 1)
+    crowned = base + 2 + NLON - 1 + EARLY * NX * NLAT
+
+    @pl.when(is_top & is_early)
+    def _():
+        pl.semaphore_wait(barrier, crowned - 1)
+
+    @pl.when(is_top & (lon_z >= EARLY))
+    def _():
+        pl.semaphore_wait(barrier, crowned)
 
     @pl.when(is_low)
     def _():
@@ -241,10 +263,6 @@
     def settle(ref, sem):
         pltpu.make_async_copy(ref, ref, sem).wait()
 
-    @pl.when(is_top)
-    def _():
-        spread(own2.at[0:FOLD2, :], fold2.at[lon, 0:FOLD2, :], 0, ring)
-
     to_east.start()
     to_west.start()
 
@@ -257,6 +275,10 @@
     def _():
         for send in south_sends:
             send.start()
+
+    @pl.when(is_top)
+    def _():
+        spread(own2.at[0:FOLD2, :], fold2.at[lon, 0:FOLD2, :], 0, ring)
 
     to_east3.start()
     to_west3.start()
@@ -310,6 +332,69 @@
 
     def turn(tile):
         return jnp.take_along_axis(tile, index, axis=1)
+
+    full = EDGE + ROWS + EDGE
+    rows_end = jnp.where(is_top, EDGE + ROWS, full)
+    pairs = ((0, 0), (0, 1), (1, 1), (1, 2), (2, 2), (2, 3))
+
+    def north_of(a):
+        return pltpu.roll(a, a.shape[0] - 1, 0)
+
+    def south_of(a):
+        return pltpu.roll(a, 1, 0)
+
+    def krylov(low, count):
+        lane = lane_iota(count)
+        first_lane = lane == 0
+        last_lane = lane == LANES - 1
+        part = slice(low, low + count)
+
+        def plus_east(a, b):
+            return (
+                pltpu.roll(jnp.where(first_lane, b, a), LANES - 1, 1),
+                pltpu.roll(jnp.where(first_lane, a, b), LANES - 1, 1),
+            )
+
+        def plus_west(a, b):
+            return (
+                pltpu.roll(jnp.where(last_lane, b, a), 1, 1),
+                pltpu.roll(jnp.where(last_lane, a, b), 1, 1),
+            )
+
+        row = lax.broadcasted_iota(jnp.int32, (count, LANES), 0) + low
+        scale2 = (x[3, 0, part, :], x[3, 1, part, :])
+        q2 = (x[0, 0, part, :], x[0, 1, part, :])
+        q_e = plus_east(*q2)
+        q_w = plus_west(*q2)
+        flow_e, flow_n = [], []
+        for h in range(2):
+            wet = scale2[h] > 0.0
+            flow_e.append(jnp.where(wet, x[1, h, part, :] - 0.05 * (q_e[h] - q_w[h]), 0.0))
+            slope = north_of(q2[h]) - south_of(q2[h])
+            flow_n.append(jnp.where(wet & (row <= rows_end), x[2, h, part, :] - 0.05 * slope, 0.0))
+        f_e = plus_east(*flow_e)
+        f_w = plus_west(*flow_e)
+        v = tuple(
+            x[4, h, part, :]
+            - scale2[h] * (0.5 * (f_e[h] - f_w[h] + north_of(flow_n[h]) - south_of(flow_n[h])))
+            for h in range(2)
+        )
+        basis = [v[0]]
+        for _ in range(3):
+            v_e = plus_east(*v)
+            v_w = plus_west(*v)
+            v = tuple(scale2[h] * (v_e[h] + v_w[h] + north_of(v[h]) + south_of(v[h])) for h in range(2))
+            basis.append(v[0])
+        return basis
+
+    basis = [v[own] for v in krylov(0, full)]
+    for i in range(3):
+        press[i, own, :] = basis[i]
+    bulk = []
+    for j, (l, r) in enumerate(pairs):
+        product = ((diagonal * basis[l]) * basis[r]).reshape(ROWS // EDGE, EDGE, LANES)
+        bulk.append(jnp.sum(product[:-1], axis=0))
+        rim[j] = product[-1]
 
     @pl.when(is_top)
     def _():
@@ -332,69 +417,45 @@
             x[3, half, north:north + 1, :] = tiles[0][7:8]
             x[3, half, north + 1:north + 3, :] = tiles[1][0:2]
             x[4, half, north:north + 3, :] = tiles[1][2:5]
-
-    full = EDGE + ROWS + EDGE
-    first_lane = lanes_w == 0
-    last_lane = lanes_w == LANES - 1
-
-    def plus_east(a, b):
-        return (
-            pltpu.roll(jnp.where(first_lane, b, a), LANES - 1, 1),
-            pltpu.roll(jnp.where(first_lane, a, b), LANES - 1, 1),
-        )
-
-    def plus_west(a, b):
-        return (
-            pltpu.roll(jnp.where(last_lane, b, a), 1, 1),
-            pltpu.roll(jnp.where(last_lane, a, b), 1, 1),
-        )
-
-    def north_of(a):
-        return pltpu.roll(a, full - 1, 0)
-
-    def south_of(a):
-        return pltpu.roll(a, 1, 0)
-
-    scale2 = (x[3, 0], x[3, 1])
-    wet2 = (scale2[0] > 0.0, scale2[1] > 0.0)
-    q2 = (x[0, 0], x[0, 1])
-    q_e = plus_east(*q2)
-    q_w = plus_west(*q2)
-    flow_e, flow_n = [], []
-    rows_w = lax.broadcasted_iota(jnp.int32, (full, LANES), 0)
-    rows_end = jnp.where(is_top, EDGE + ROWS, full)
-    for h in range(2):
-        flow_e.append(jnp.where(wet2[h], x[1, h] - 0.05 * (q_e[h] - q_w[h]), 0.0))
-        flow_n.append(jnp.where(wet2[h] & (rows_w <= rows_end), x[2, h] - 0.05 * (north_of(q2[h]) - south_of(q2[h])), 0.0))
-    f_e = plus_east(*flow_e)
-    f_w = plus_west(*flow_e)
-    basis = []
-    v = tuple(
-        x[4, h] - scale2[h] * (0.5 * (f_e[h] - f_w[h] + north_of(flow_n[h]) - south_of(flow_n[h])))
-        for h in range(2)
-    )
-    basis.append(v[0][EDGE:EDGE + ROWS])
-    for _ in range(3):
-        v_e = plus_east(*v)
-        v_w = plus_west(*v)
-        v = tuple(scale2[h] * (v_e[h] + v_w[h] + north_of(v[h]) + south_of(v[h])) for h in range(2))
-        basis.append(v[0][EDGE:EDGE + ROWS])
-
-    for i in range(3):
-        press[i, own, :] = basis[i]
+        final = slice(EDGE, 2 * EDGE)
+        rim_diagonal = 4.0 + ebuf[0, ROWS - EDGE:, :]
+        basis = [v[final] for v in krylov(ROWS - EDGE, 3 * EDGE)]
+        for i in range(3):
+            press[i, ROWS:ROWS + EDGE, :] = basis[i]
+        for j, (l, r) in enumerate(pairs):
+            rim[j] = (rim_diagonal * basis[l]) * basis[r]
+
     sub = lax.broadcasted_iota(jnp.int32, (EDGE, LANES), 0)
     table = jnp.zeros((EDGE, LANES), jnp.float32)
-    for j, (l, r) in enumerate(((0, 0), (0, 1), (1, 1), (1, 2), (2, 2), (2, 3))):
-        product = (diagonal * basis[l]) * basis[r]
-        line = jnp.sum(product.reshape(ROWS // EDGE, EDGE, LANES), axis=0)
-        line = jnp.sum(line, axis=0, keepdims=True)
+    for j in range(len(pairs)):
+        line = jnp.sum(bulk[j] + rim[j], axis=0, keepdims=True)
         table = jnp.where(sub == j, line, table)
     table = jnp.sum(table, axis=1, keepdims=True)
     message = jnp.sum(jnp.where(sub == lanes_e, table, 0.0), axis=0, keepdims=True)
     vec[0:1, :] = message
-    mine1 = lon_x * NLAT + lat
-    sums1[pl.ds(mine1, 1), :] = message
-    spread(vec.at[0:1, :], sums1.at[pl.ds(mine1, 1), :], 2, near)
+    mine1 = lon_x * (NLAT - 1) + lat
+
+    @pl.when(not_top)
+    def _():
+        sums1[pl.ds(mine1, 1), :] = message
+        spread(vec.at[0:1, :], sums1.at[pl.ds(mine1, 1), :], 2, near)
+
+    @pl.when(is_top)
+    def _():
+        late1[pl.ds(lon_x, 1), :] = message
+        for dz in range(NZ):
+            for dx, dy, dc in itertools.product(range(NX), range(NLAT // 2), range(2)):
+                if dz or dx or dy or dc:
+
+                    @pl.when(zs[dz] < EARLY * NX)
+                    def _(dev=at(dz, dx, dy, dc)):
+                        spread(vec.at[0:1, :], crown.at[pl.ds(lon, 1), :], 5, [dev])
+
+        spread(vec.at[0:1, :], late1.at[pl.ds(lon_x, 1), :], 6, near)
+
+    @pl.when(is_top & is_early)
+    def _():
+        crown[pl.ds(lon, 1), :] = message
 
     @pl.when(is_top)
     def _():
@@ -467,12 +528,49 @@
 
     update(0, ROWS, 2)
 
-    settle(sums1.at[0:NX * NLAT - 1, :], group_recv.at[2])
+    body_rows = NX * (NLAT - 1)
+
+    @pl.when(is_top)
+    def _():
+        settle(sums1, group_recv.at[2])
+
+    @pl.when(not_top)
+    def _():
+        settle(sums1.at[0:body_rows - 1, :], group_recv.at[2])
+
     total = jnp.sum(sums1[...], axis=0, keepdims=True)
-    mine2 = lon_z
     vec[EDGE:EDGE + 1, :] = total
-    sums2[pl.ds(mine2, 1), :] = total
-    spread(vec.at[EDGE:EDGE + 1, :], sums2.at[pl.ds(mine2, 1), :], 3, far)
+
+    @pl.when(is_early)
+    def _():
+        sums2[pl.ds(lon_z, 1), :] = total
+
+    def cross(row, early):
+        for dz in sorted(range(1, NZ), key=lambda o: -hops(o, NZ)):
+            bound = EARLY * NX
+
+            @pl.when((zs[dz] < bound) if early else (zs[dz] >= bound))
+            def _(dev=at(dz, 0, 0, 0)):
+                spread(vec.at[row:row + 1, :], sums2.at[pl.ds(lon_z, 1), :], 3, [dev])
+
+    cross(EDGE, True)
+
+    @pl.when(is_top)
+    def _():
+        settle(late1.at[0:NX - 1, :], group_recv.at[6])
+
+    @pl.when(not_top)
+    def _():
+        settle(late1, group_recv.at[6])
+
+    total = total + jnp.sum(late1[...], axis=0, keepdims=True)
+    vec[EDGE + 1:EDGE + 2, :] = total
+
+    @pl.when(lon_z >= EARLY)
+    def _():
+        sums2[pl.ds(lon_z, 1), :] = total
+
+    cross(EDGE + 1, False)
 
     beside = [(lon - lon_x + lax.rem(lon_x + k, NX), lat) for k in range(1, NX)]
     kept = lane_iota(FOLD3) <= offset
@@ -489,7 +587,21 @@
         spread(own3x, foldx.at[lon_x], 4, beside)
 
     settle(sums2.at[0:NZ - 1, :], group_recv.at[3])
-    total = jnp.sum(sums2[...], axis=0, keepdims=True)
+    vec[EDGE + 2:EDGE + 3, :] = jnp.sum(sums2[...], axis=0, keepdims=True)
+
+    @pl.when(is_early & is_top)
+    def _():
+        settle(crown.at[0:NLON - 1, :], group_recv.at[5])
+
+    @pl.when(is_early & not_top)
+    def _():
+        settle(crown, group_recv.at[5])
+
+    @pl.when(is_early)
+    def _():
+        vec[EDGE + 2:EDGE + 3, :] = vec[EDGE + 2:EDGE + 3, :] + jnp.sum(crown[...], axis=0, keepdims=True)
+
+    total = vec[EDGE + 2:EDGE + 3, :]
     mu = [total[:, j:j + 1] for j in range(6)]
 
     def gram(a, b, shift):
@@ -553,7 +665,22 @@
         settle(foldz.at[0:NZ - 1], group_send.at[1])
         settle(foldx.at[0:NX - 1], group_send.at[4])
 
-    settle(sums1.at[0:NX * NLAT - 1, :], group_send.at[2])
+    @pl.when(is_top & is_early)
+    def _():
+        settle(wide_sent.at[0:EARLY * NX * NLAT - 1, :], group_send.at[5])
+
+    @pl.when(is_top & (lon_z >= EARLY))
+    def _():
+        settle(wide_sent, group_send.at[5])
+
+    @pl.when(is_top)
+    def _():
+        settle(wide_sent.at[0:NX * NLAT - 1, :], group_send.at[6])
+
+    @pl.when(not_top)
+    def _():
+        settle(wide_sent.at[0:NX * NLAT - 1, :], group_send.at[2])
+
     settle(sums2.at[0:NZ - 1, :], group_send.at[3])
 
 
@@ -599,16 +726,20 @@
             pltpu.VMEM((FOLD3, LANES), f32),
             pltpu.VMEM((NX, FOLD3, LANES), f32),
             pltpu.VMEM((3, full, LANES), f32),
+            pltpu.VMEM((6, EDGE, LANES), f32),
             pltpu.VMEM((2 * EDGE, LANES), f32),
-            pltpu.VMEM((NX * NLAT, LANES), f32),
+            pltpu.VMEM((NX * (NLAT - 1), LANES), f32),
             pltpu.VMEM((NZ, LANES), f32),
+            pltpu.VMEM((NX, LANES), f32),
+            pltpu.VMEM((NLON, LANES), f32),
+            pltpu.VMEM((EARLY * NX * NLAT, LANES), f32),
             pltpu.SMEM((LEVELS,), f32),
             pltpu.SMEM((LANES,), jnp.int32),
             pltpu.SemaphoreType.DMA((9,)),
             pltpu.SemaphoreType.DMA((12,)),
             pltpu.SemaphoreType.DMA((12,)),
-            pltpu.SemaphoreType.DMA((5,)),
-            pltpu.SemaphoreType.DMA((5,)),
+            pltpu.SemaphoreType.DMA((7,)),
+            pltpu.SemaphoreType.DMA((7,)),
         ],
         compiler_params=pltpu.CompilerParams(
             collective_id=0, has_side_effects=True, vmem_limit_bytes=40 * 1024 * 1024

time: 27.7 us -> 26.6 us (0.960)
  Pallas kernels: 26.9 us -> 25.8 us
    pallas_call x1, Pallas kernels: 25.8 us -> 24.7 us  [body(): pl.pallas_call(kernel, out_shape=shapes, in_specs=[hbm] * 9, out_specs=[v...]
where the time goes in v6:
time: 26.6 us; the launch traced here: 26.4 us
  Pallas kernels  25.8 us (97%)
  between operations  0.64 us (2%)
    pallas_call x1, Pallas kernels, body(): pl.pallas_call(kernel, out_shape=shapes, in_specs=[hbm] * 9, out_specs=[v...  24.7 us
    pallas_call x1, Pallas kernels, body(): pl.pallas_call(store, out_shape=shapes, in_specs=[anyspec] * 5, out_specs...  1.1 us

profile of v6, /device:TPU:1, one launch (start us, length us, event | category | flops | bytes accessed | tf_op | source)
XLA Modules:
  0.0 26.4 jit_solution(6746697178744057884)
XLA Ops:
  0.6 24.7 %shard_map.128 = (f32[10,64,128]{2,1,0:T(8,128)S(1)}, f32[10,64,128]{2,1,0:T(8,128)S(1)}, f32[10,64,128]{2,1,0:T(8,128)S(1)}, f32[10,64,128]{2,1,0:T(8,128)S(1)}, f32[64,128]{1,0:T(8,128)S(1)}) custom-call(f32[10,64,128]{2,1,0:T(8,128)} %t_hbm.1, f32[10,64,128]{2,1,0:T(8,128)} %s_hbm.1, f32[10,64,128]{2,1,0:T(8,128)} %u_hbm.1, f32[10,64,128]{2,1,0:T(8,128)} %v_hbm.1, ...), custom_call_target="tpu_custom_call" | custom-call | tf_op jit(solution)/shard_map/pallas_call | solution.py:705
  25.3 1.1 %shard_map.129 = (f32[10,64,128]{2,1,0:T(8,128)}, f32[10,64,128]{2,1,0:T(8,128)}, f32[10,64,128]{2,1,0:T(8,128)}, f32[10,64,128]{2,1,0:T(8,128)}, f32[64,128]{1,0:T(8,128)}) custom-call(f32[10,64,128]{2,1,0:T(8,128)S(1)} %get-tuple-element.10.refs_0_, f32[10,64,128]{2,1,0:T(8,128)S(1)} %get-tuple-element.11.refs_1_, ...), custom_call_target="tpu_custom_call" | custom-call | tf_op jit(solution)/shard_map/pallas_call | solution.py:749

commit v7 on v6

--- a/solution.py
+++ b/solution.py
@@ -16,7 +16,7 @@
 NLAT = 8
 NX = 4
 NZ = 8
-EARLY = 2
+EARLY = 4
 SPAN2 = 10
 SPAN3 = 4
 FOLD2 = 13
@@ -290,6 +290,10 @@
     @pl.when(not_low)
     def _():
         to_south3.start()
+
+    @pl.when(is_top)
+    def _():
+        spread(own3, foldz.at[lon_z], 1, far)
 
     to_east.wait_recv()
     to_west.wait_recv()
@@ -457,20 +461,17 @@
     def _():
         crown[pl.ds(lon, 1), :] = message
 
-    @pl.when(is_top)
-    def _():
-        spread(own3, foldz.at[lon_z], 1, far)
-
-    to_east3.wait_recv()
-    to_west3.wait_recv()
-
-    @pl.when(not_low)
-    def _():
-        to_north3.wait_recv()
-
-    @pl.when(not_top)
-    def _():
-        to_south3.wait_recv()
+    def hear_tracers():
+        to_east3.wait_recv()
+        to_west3.wait_recv()
+
+        @pl.when(not_low)
+        def _():
+            to_north3.wait_recv()
+
+        @pl.when(not_top)
+        def _():
+            to_south3.wait_recv()
 
     def update(low, rows, parts):
         lane = lane_iota(rows)
@@ -526,7 +527,10 @@
                 p_w = pltpu.roll(jnp.where(lane == LANES - 1, level_side, centre), 1, 1)
                 nu[k, part, :] = wet * (u - 0.05 * (p_e - p_w))
 
-    update(0, ROWS, 2)
+    @pl.when(not_top)
+    def _():
+        hear_tracers()
+        update(0, ROWS, 2)
 
     body_rows = NX * (NLAT - 1)
 
@@ -585,6 +589,8 @@
         own3x[...] = joint
         foldx[lon_x] = joint
         spread(own3x, foldx.at[lon_x], 4, beside)
+        hear_tracers()
+        update(0, ROWS, 2)
 
     settle(sums2.at[0:NZ - 1, :], group_recv.at[3])
     vec[EDGE + 2:EDGE + 3, :] = jnp.sum(sums2[...], axis=0, keepdims=True)

time: 26.6 us -> 26.2 us (0.985)
  Pallas kernels: 25.8 us -> 25.4 us
    pallas_call x1, Pallas kernels: 24.7 us -> 24.3 us  [body(): pl.pallas_call(kernel, out_shape=shapes, in_specs=[hbm] * 9, out_specs=[v...]
where the time goes in v7:
time: 26.2 us; the launch traced here: 26.1 us
  Pallas kernels  25.4 us (97%)
  between operations  0.64 us (2%)
    pallas_call x1, Pallas kernels, body(): pl.pallas_call(kernel, out_shape=shapes, in_specs=[hbm] * 9, out_specs=[v...  24.3 us
    pallas_call x1, Pallas kernels, body(): pl.pallas_call(store, out_shape=shapes, in_specs=[anyspec] * 5, out_specs...  1.1 us

profile of v7, /device:TPU:1, one launch (start us, length us, event | category | flops | bytes accessed | tf_op | source)
XLA Modules:
  0.0 26.1 jit_solution(10693712663032964693)
XLA Ops:
  0.6 24.3 %shard_map.128 = (f32[10,64,128]{2,1,0:T(8,128)S(1)}, f32[10,64,128]{2,1,0:T(8,128)S(1)}, f32[10,64,128]{2,1,0:T(8,128)S(1)}, f32[10,64,128]{2,1,0:T(8,128)S(1)}, f32[64,128]{1,0:T(8,128)S(1)}) custom-call(f32[10,64,128]{2,1,0:T(8,128)} %t_hbm.1, f32[10,64,128]{2,1,0:T(8,128)} %s_hbm.1, f32[10,64,128]{2,1,0:T(8,128)} %u_hbm.1, f32[10,64,128]{2,1,0:T(8,128)} %v_hbm.1, ...), custom_call_target="tpu_custom_call" | custom-call | tf_op jit(solution)/shard_map/pallas_call | solution.py:711
  25.0 1.1 %shard_map.129 = (f32[10,64,128]{2,1,0:T(8,128)}, f32[10,64,128]{2,1,0:T(8,128)}, f32[10,64,128]{2,1,0:T(8,128)}, f32[10,64,128]{2,1,0:T(8,128)}, f32[64,128]{1,0:T(8,128)}) custom-call(f32[10,64,128]{2,1,0:T(8,128)S(1)} %get-tuple-element.10.refs_0_, f32[10,64,128]{2,1,0:T(8,128)S(1)} %get-tuple-element.11.refs_1_, ...), custom_call_target="tpu_custom_call" | custom-call | tf_op jit(solution)/shard_map/pallas_call | solution.py:755

commit v8 on v7

--- a/solution.py
+++ b/solution.py
@@ -43,6 +43,8 @@
     lon_z = lax.div(lon, NX)
     east = lax.rem(lon + 1, NLON)
     west = lax.rem(lon + NLON - 1, NLON)
+    above = lax.rem(lat + 1, NLAT)
+    beneath = lax.rem(lat + NLAT - 1, NLAT)
     is_top = lat == NLAT - 1
     is_low = lat == 0
     not_top = lat < NLAT - 1
@@ -107,13 +109,13 @@
 
     @pl.when(not_top)
     def _():
-        greet((east, lat + 1))
-        greet((west, lat + 1))
+        greet((east, above))
+        greet((west, above))
 
     @pl.when(not_low)
     def _():
-        greet((east, lat - 1))
-        greet((west, lat - 1))
+        greet((east, beneath))
+        greet((west, beneath))
 
     loads = [
         pltpu.make_async_copy(w_hbm, wbuf, in_sem.at[0]),
@@ -236,19 +238,19 @@
     top_rows = slice(EDGE + ROWS, EDGE + ROWS + EDGE)
     to_east = copy(slim.at[0], heard.at[0], 0, (east, lat))
     to_west = copy(slim.at[1], heard.at[1], 1, (west, lat))
-    to_north = copy(x.at[:, 0, ROWS:EDGE + ROWS, :], x.at[:, 0, 0:EDGE, :], 2, (lon, lat + 1))
-    to_ne = copy(pack.at[ROWS - EDGE:ROWS, :], wide.at[0, 0], 3, (east, lat + 1))
-    to_nw = copy(pack.at[ROWS - EDGE:ROWS, :], wide.at[1, 0], 4, (west, lat + 1))
-    to_south = copy(x.at[:, 0, EDGE:2 * EDGE, :], x.at[:, 0, top_rows, :], 5, (lon, lat - 1))
-    to_se = copy(pack.at[0:EDGE, :], wide.at[0, 1], 6, (east, lat - 1))
-    to_sw = copy(pack.at[0:EDGE, :], wide.at[1, 1], 7, (west, lat - 1))
+    to_north = copy(x.at[:, 0, ROWS:EDGE + ROWS, :], x.at[:, 0, 0:EDGE, :], 2, (lon, above))
+    to_ne = copy(pack.at[ROWS - EDGE:ROWS, :], wide.at[0, 0], 3, (east, above))
+    to_nw = copy(pack.at[ROWS - EDGE:ROWS, :], wide.at[1, 0], 4, (west, above))
+    to_south = copy(x.at[:, 0, EDGE:2 * EDGE, :], x.at[:, 0, top_rows, :], 5, (lon, beneath))
+    to_se = copy(pack.at[0:EDGE, :], wide.at[0, 1], 6, (east, beneath))
+    to_sw = copy(pack.at[0:EDGE, :], wide.at[1, 1], 7, (west, beneath))
     to_east3 = copy(pack3.at[0], wide3.at[0], 8, (east, lat))
     to_west3 = copy(pack3.at[1], wide3.at[1], 9, (west, lat))
     to_north3 = copy(
-        ts.at[:, :, EDGE + ROWS - 2:EDGE + ROWS, :], ts.at[:, :, EDGE - 2:EDGE, :], 10, (lon, lat + 1)
+        ts.at[:, :, EDGE + ROWS - 2:EDGE + ROWS, :], ts.at[:, :, EDGE - 2:EDGE, :], 10, (lon, above)
     )
     to_south3 = copy(
-        ts.at[:, :, EDGE:EDGE + 2, :], ts.at[:, :, EDGE + ROWS:EDGE + ROWS + 2, :], 11, (lon, lat - 1)
+        ts.at[:, :, EDGE:EDGE + 2, :], ts.at[:, :, EDGE + ROWS:EDGE + ROWS + 2, :], 11, (lon, beneath)
     )
     north_sends = (to_north, to_ne, to_nw)
     south_sends = (to_south, to_se, to_sw)

time: 26.2 us -> 26.2 us (level)
  no operation moved by 1% of the time
where the time goes in v8:
time: 26.2 us; the launch traced here: 26.1 us
  Pallas kernels  25.5 us (97%)
  between operations  0.64 us (2%)
    pallas_call x1, Pallas kernels, body(): pl.pallas_call(kernel, out_shape=shapes, in_specs=[hbm] * 9, out_specs=[v...  24.4 us
    pallas_call x1, Pallas kernels, body(): pl.pallas_call(store, out_shape=shapes, in_specs=[anyspec] * 5, out_specs...  1.1 us

profile of v8, /device:TPU:1, one launch (start us, length us, event | category | flops | bytes accessed | tf_op | source)
XLA Modules:
  0.0 26.1 jit_solution(7188574281179350368)
XLA Ops:
  0.6 24.4 %shard_map.128 = (f32[10,64,128]{2,1,0:T(8,128)S(1)}, f32[10,64,128]{2,1,0:T(8,128)S(1)}, f32[10,64,128]{2,1,0:T(8,128)S(1)}, f32[10,64,128]{2,1,0:T(8,128)S(1)}, f32[64,128]{1,0:T(8,128)S(1)}) custom-call(f32[10,64,128]{2,1,0:T(8,128)} %t_hbm.1, f32[10,64,128]{2,1,0:T(8,128)} %s_hbm.1, f32[10,64,128]{2,1,0:T(8,128)} %u_hbm.1, f32[10,64,128]{2,1,0:T(8,128)} %v_hbm.1, ...), custom_call_target="tpu_custom_call" | custom-call | tf_op jit(solution)/shard_map/pallas_call | solution.py:713
  25.0 1.1 %shard_map.129 = (f32[10,64,128]{2,1,0:T(8,128)}, f32[10,64,128]{2,1,0:T(8,128)}, f32[10,64,128]{2,1,0:T(8,128)}, f32[10,64,128]{2,1,0:T(8,128)}, f32[64,128]{1,0:T(8,128)}) custom-call(f32[10,64,128]{2,1,0:T(8,128)S(1)} %get-tuple-element.10.refs_0_, f32[10,64,128]{2,1,0:T(8,128)S(1)} %get-tuple-element.11.refs_1_, ...), custom_call_target="tpu_custom_call" | custom-call | tf_op jit(solution)/shard_map/pallas_call | solution.py:757
